TPU v7x, 32 devices: a whole 2x2x4 slice. The times are simulated.
32 devices in a mesh: groups: 2 (over x), ctx: 2 (over core), tp: 8 (over z, y).
Axes of the slice: x: 2, y: 2, z: 4, core: 2. Of those that a mesh axis runs over, the one named last changes fastest.
Arguments:
- hidden_in: bfloat16 [2048, 8192], P(('groups', 'ctx'), 'tp'), parts along dimension 0, may hold values from -20 to 20
- attn_gain: bfloat16 [8192], replicated, may hold values from 0.5 to 1.5
- query_weight: bfloat16 [8192, 4096], P(None, 'tp'), may hold values from -0.0625 to 0.0625
- keys: bfloat16 [16384, 512], P(('groups', 'ctx')), parts along dimension 0, may hold values from -300 to 300
- values: bfloat16 [16384, 512], P(('groups', 'ctx')), parts along dimension 0, may hold values from -6 to 6
- offset: int32 [2], P('groups'), parts along dimension 0, may hold values from 4096 to 7168
- out_weight: bfloat16 [4096, 8192], P('tp'), may hold values from -1 to 1
- sign_bits: int32 [8192], replicated, may hold values from 0 to 1
- attn_exps: int32 [64, 64], P(('groups', 'ctx')), parts along dimension 0, may hold values from -8 to -5
- norm_gain: bfloat16 [8192], replicated, may hold values from 0.25 to 1.75
- norm_exps: int32 [64, 64], P(('groups', 'ctx')), parts along dimension 0, may hold values from -6 to -4
Outputs:
- normed: bfloat16 [2048, 8192], P(('groups', 'ctx')), parts along dimension 0
There are 2 independent parts, one for each index of `groups`. A program takes and returns all parts, laid end to end along the dimension named above; an argument that names none is the same for every part. Nothing has to cross between parts.
Inputs may be any that keep to these rules, and one draw needn't show every extreme that they name: `offset`: every query row sees all of the first 4096 context positions.
All inputs are finite; a program needn't handle non-finite values.
Results may differ from a plain program's by a relative error of at most 0.014.
The roundings to bfloat16 on the way count: a program that leaves them out, or rounds other values in their place, can miss the bound.
Values may be sent and summed in bfloat16 or wider, within the bound.
No kernel may reach another device: no remote copies, remote signals or barrier semaphores. Data moves between devices by JAX's collectives and lax.ppermute only.
A program may use at most 256 MiB of HBM per device.

v0:
```python
import math

import jax
import jax.numpy as jnp
from jax import lax
from jax.sharding import PartitionSpec as P

D = 8192
HD = 128
HEADS = 32
KVH = 4
HB = 128
RB = 32


def shifted(value, axis, steps):
    count = lax.axis_size(axis)
    pairs = [(source, (source + steps) % count) for source in range(count)]
    return lax.ppermute(value, axis, pairs)


def hadamard_table(order):
    table = jnp.ones((1, 1), dtype=jnp.float32)
    while table.shape[0] < order:
        upper = jnp.concatenate([table, table], axis=1)
        lower = jnp.concatenate([table, -table], axis=1)
        table = jnp.concatenate([upper, lower], axis=0)
    return table


def rotary(vectors, positions):
    half_dim = vectors.shape[-1] // 2
    inv_freq = jnp.exp(
        -(jnp.arange(half_dim, dtype=jnp.float32) * (2.0 / vectors.shape[-1])) * math.log(500000.0)
    )
    angles = positions.astype(jnp.float32)[:, None] * inv_freq[None, :]
    cosine = jnp.cos(angles)
    sine_vals = jnp.sin(angles)
    first_half = vectors[..., :half_dim]
    second_half = vectors[..., half_dim:]
    return jnp.concatenate(
        [
            first_half * cosine - second_half * sine_vals,
            second_half * cosine + first_half * sine_vals,
        ],
        axis=-1,
    )


def encode(partial_value, sign_vector, exps, hadamard):
    row_count = partial_value.shape[0]
    blocks = (partial_value * sign_vector).reshape(row_count, -1, hadamard.shape[0])
    spun = jnp.einsum("rbi,ij->rbj", blocks, hadamard, precision=lax.Precision.HIGHEST) * (
        1.0 / math.sqrt(hadamard.shape[0])
    )
    coded = jnp.clip(spun * jnp.exp2(-exps.astype(jnp.float32))[..., None], -127.0, 127.0)
    return coded.reshape(row_count, -1)


def decode(summed, sign_vector, exps, hadamard):
    row_count = summed.shape[0]
    blocks = (
        summed.reshape(row_count, -1, hadamard.shape[0])
        * jnp.exp2(exps.astype(jnp.float32))[..., None]
    )
    spun = jnp.einsum("rbi,ij->rbj", blocks, hadamard, precision=lax.Precision.HIGHEST) * (
        1.0 / math.sqrt(hadamard.shape[0])
    )
    return spun.reshape(row_count, -1) * sign_vector


def attend_block(queries, key_block, value_block, query_pos, key_pos):
    scores = jnp.einsum("hqd,sd->hqs", queries, key_block, preferred_element_type=jnp.float32) * (
        1.0 / math.sqrt(HD)
    )
    visible = (key_pos[None, :] <= query_pos[:, None])[None]
    scores = jnp.where(visible, scores, -1e30)
    maxima = jnp.max(scores, axis=2)
    weights_f = jnp.where(visible, jnp.exp(scores - maxima[..., None]), 0.0)
    totals = jnp.sum(weights_f, axis=2)
    accumulated = jnp.einsum(
        "hqs,sd->hqd",
        weights_f.astype(jnp.bfloat16),
        value_block,
        preferred_element_type=jnp.float32,
    )
    return (accumulated, maxima, totals)


def code_norm(scaled, exps):
    row_count = scaled.shape[0]
    coded = jnp.clip(
        scaled.reshape(row_count, -1, HB) * jnp.exp2(-exps.astype(jnp.float32))[..., None],
        -127.0,
        127.0,
    )
    return coded.astype(jnp.bfloat16).reshape(row_count, -1)


def local(
    hidden_in,
    attn_gain,
    query_weight,
    keys,
    values,
    offset,
    out_weight,
    sign_bits,
    attn_exps,
    norm_gain,
    norm_exps,
):
    gathered = lax.all_gather(hidden_in, "tp", axis=1, tiled=True)
    features = gathered.astype(jnp.float32)
    mean_in = jnp.sum(features * features, axis=1, keepdims=True) / D
    normed_in = (features * lax.rsqrt(mean_in + 1e-05) * attn_gain.astype(jnp.float32)).astype(
        jnp.bfloat16
    )
    projected_q = jnp.dot(normed_in, query_weight, preferred_element_type=jnp.float32)
    row_count = gathered.shape[0]
    heads_dev = query_weight.shape[1] // HD
    ctx_count = lax.axis_size("ctx")
    ctx_index = lax.axis_index("ctx")
    tp_index = lax.axis_index("tp")
    row_iota = jnp.arange(row_count, dtype=jnp.int32)
    query_pos = offset[0] + ctx_index * row_count + row_iota
    rotated = rotary(
        projected_q.reshape(row_count, heads_dev, HD).transpose(1, 0, 2), query_pos
    ).astype(jnp.bfloat16)
    block_len = keys.shape[0]
    block_iota = jnp.arange(block_len, dtype=jnp.int32)
    column = tp_index * heads_dev // (HEADS // KVH) * HD
    own_keys = lax.dynamic_slice_in_dim(keys, column, HD, 1)
    own_values = lax.dynamic_slice_in_dim(values, column, HD, 1)
    own_pos = ctx_index * block_len + block_iota
    prior = (ctx_index + ctx_count - 1) % ctx_count
    nearby = attend_block(rotated, own_keys, own_values, query_pos, own_pos)
    other_keys, other_values = shifted((own_keys, own_values), "ctx", 1)
    remote = attend_block(
        rotated, other_keys, other_values, query_pos, prior * block_len + block_iota
    )
    overall = jnp.maximum(nearby[1], remote[1])
    near_factor = jnp.exp(nearby[1] - overall)
    remote_factor = jnp.exp(remote[1] - overall)
    numerator = near_factor[..., None] * nearby[0] + remote_factor[..., None] * remote[0]
    denominator = near_factor * nearby[2] + remote_factor * remote[2]
    mixed = (numerator / denominator[..., None]).astype(jnp.bfloat16)
    attended = mixed.transpose(1, 0, 2).reshape(row_count, heads_dev * HD)
    hadamard = hadamard_table(HB)
    sign_vector = (2 * sign_bits - 1).astype(jnp.float32)
    e_rows = jnp.repeat(attn_exps, RB, axis=0)
    norm_rows = jnp.repeat(norm_exps, RB, axis=0)
    partial_value = jnp.dot(attended, out_weight, preferred_element_type=jnp.float32)
    codes = encode(partial_value, sign_vector, e_rows, hadamard)
    summed = lax.psum_scatter(
        codes.astype(jnp.bfloat16), "tp", scatter_dimension=1, tiled=True
    ).astype(jnp.float32)
    col_width = summed.shape[1]
    col_start = tp_index * col_width
    local_blocks = col_width // HB
    local_e = lax.dynamic_slice_in_dim(e_rows, tp_index * local_blocks, local_blocks, 1)
    local_sign = lax.dynamic_slice_in_dim(sign_vector, col_start, col_width, 0)
    projected = decode(summed, local_sign, local_e, hadamard)
    residual = (hidden_in.astype(jnp.float32) + projected).astype(jnp.bfloat16)
    resid_f = residual.astype(jnp.float32)
    squares = lax.psum(jnp.sum(resid_f * resid_f, axis=1), "tp")
    mean_sq = squares[:, None] / D
    local_gain = lax.dynamic_slice_in_dim(norm_gain, col_start, col_width, 0).astype(jnp.float32)
    scaled = resid_f * lax.rsqrt(mean_sq + 1e-05) * local_gain
    local_f = lax.dynamic_slice_in_dim(norm_rows, tp_index * local_blocks, local_blocks, 1)
    norm_code = code_norm(scaled, local_f)
    whole_code = lax.all_gather(norm_code, "tp", axis=1, tiled=True)
    decoded = (
        whole_code.reshape(row_count, -1, HB).astype(jnp.float32)
        * jnp.exp2(norm_rows.astype(jnp.float32))[..., None]
    )
    return decoded.reshape(row_count, -1).astype(jnp.bfloat16)


def solution(mesh):
    return jax.shard_map(
        local,
        mesh=mesh,
        in_specs=(
            P(("groups", "ctx"), "tp"),
            P(),
            P(None, "tp"),
            P(("groups", "ctx"), None),
            P(("groups", "ctx"), None),
            P("groups"),
            P("tp", None),
            P(),
            P(("groups", "ctx"), None),
            P(),
            P(("groups", "ctx"), None),
        ),
        out_specs=P(("groups", "ctx"), None),
        check_vma=False,
    )
```

profile of v0, /device:TPU:0, one launch (start us, length us, event | category | flops | bytes accessed | tf_op | source)
XLA Modules:
  0.0 609.2 jit_solution(16392114887534224990)
XLA Ops:
  6.5 0.0 all-gather.3.cloned.1.call-start
  6.5 0.7 all-gather.3.cloned.1.call-update
  7.3 0.0 reduce-scatter.2.cloned.1.call-start
  7.3 2.3 constant_dynamic-slice_fusion.1
  9.7 0.5 collective-permute-start
  10.1 1.3 constant_dynamic-slice_fusion
  11.4 0.0 copy-start.2
  11.4 1.3 copy.39
  12.7 0.1 collective-permute-start.1
  13.5 0.7 convert_element_type.82
  14.2 0.7 broadcast_in_dim.36
  14.9 0.1 copy.30
  15.0 0.0 copy-start.4
  15.1 0.8 add_convert_fusion.2
  15.8 0.7 exponential_multiply_fusion
  16.5 1.7 multiply_cosine_fusion
  18.3 0.0 copy-done.4
  18.3 3.6 broadcast_compare_fusion
  21.8 115.4 %all-gather.3.cloned.1.call-done = bf16[512,8192]{1,0:T(8,128)(2,1)} async-done(((bf16[512,1024]{1,0:T(8,128)(2,1)}), bf16[512,8192]{1,0:T(8,128)(2,1)}) %all-gather.3.cloned.1.call-update) | async-done | bytes 8388624 | tf_op jit(solution)/shard_map/all_gather | solution.py:113
  137.3 5.1 fusion.6
  142.4 11.3 %fusion.21 = f32[512,512]{0,1:T(8,128)} fusion(bf16[8192,512]{1,0:T(8,128)(2,1)} %param.13, bf16[512,8192]{1,0:T(8,128)(2,1)} %all-gather.3.cloned.1.call-done, f32[8192]{0:T(1024)S(1)} %convert_element_type.82, f32[512]{0:T(512)S(1)} %add_rsqrt_fusion.1), kind=kOutput, calls=%fused_computation.26 | convolution fusion | flops 4311744512 | bytes 17860608 | tf_op jit(solution)/shard_map/dot_general | solution.py:119
  153.7 0.0 copy-done.2
  153.7 1.5 copy.27
  155.3 1.4 subtract_convert_fusion
  156.7 0.0 copy-start
  156.7 16.0 %fusion = (f32[4,512]{1,0:T(4,128)S(1)}, f32[4,512,4096]{2,1,0:T(8,128)}) fusion(pred[512,4096]{1,0:T(8,128)(4,1)} %get-tuple-element.15, bf16[4096,128]{1,0:T(8,128)(2,1)} %constant_dynamic-slice_fusion.1, bf16[4,512,64]{2,1,0:T(8,128)(2,1)S(1)} %get-tuple-element.11, bf16[4,512,64]{2,1,0:T(8,128)(2,1)S(1)} %get-tuple-element.10), kind=kOutput, calls=%fused_computation.4 | convolution fusion | flops 2173696000 | bytes 37232640 | tf_op jit(solution)/shard_map/hqd,sd->hqs/dot_general | solution.py:73
  172.7 0.0 copy-done
  172.7 15.7 %fusion.2 = f32[4,512]{1,0:T(4,128)S(1)} fusion(f32[4,512,4096]{2,1,0:T(8,128)} %get-tuple-element.17, f32[4,512]{1,0:T(4,128)S(1)} %get-tuple-element.16, pred[512,4096]{1,0:T(8,128)(4,1)S(1)} %copy-done), kind=kLoop, calls=%fused_computation.6 | loop fusion | flops 41940992 | bytes 35667968 | tf_op jit(solution)/shard_map/reduce_sum | solution.py:80
  188.3 0.0 collective-permute-done
  188.3 15.4 %fusion.1 = (f32[4,512]{1,0:T(4,128)S(1)}, f32[4,512,4096]{2,1,0:T(8,128)}) fusion(pred[512,4096]{1,0:T(8,128)(4,1)S(1)} %get-tuple-element.14, bf16[4096,128]{1,0:T(8,128)(2,1)} %collective-permute-done, bf16[4,512,64]{2,1,0:T(8,128)(2,1)S(1)} %get-tuple-element.11, bf16[4,512,64]{2,1,0:T(8,128)(2,1)S(1)} %get-tuple-element.10), kind=kOutput, calls=%fused_computation.5 | convolution fusion | flops 2173696000 | bytes 37232640 | tf_op jit(solution)/shard_map/hqd,sd->hqs/dot_general | solution.py:73
  203.7 0.0 copy-start.3
  203.7 15.7 %fusion.4 = f32[4,512]{1,0:T(4,128)S(1)} fusion(f32[4,512,4096]{2,1,0:T(8,128)} %get-tuple-element.19, f32[4,512]{1,0:T(4,128)S(1)} %get-tuple-element.18, pred[512,4096]{1,0:T(8,128)(4,1)S(1)} %get-tuple-element.14), kind=kLoop, calls=%fused_computation.8 | loop fusion | flops 41940992 | bytes 35667968 | tf_op jit(solution)/shard_map/reduce_sum | solution.py:80
  219.4 0.0 copy-done.3
  219.4 17.0 %fusion.41 = f32[512,4,128]{0,2,1:T(8,128)} fusion(f32[4,512,4096]{2,1,0:T(8,128)} %get-tuple-element.17, f32[4,512]{1,0:T(4,128)S(1)} %get-tuple-element.16, pred[512,4096]{1,0:T(8,128)(4,1)} %get-tuple-element.15, bf16[4096,128]{1,0:T(8,128)(2,1)S(1)} %copy-done.3, f32[512,4]{0,1:T(4,128)S(1)} %get-tuple-element.9), kind=kOutput, calls=%fused_computation.45 | convolution fusion | flops 2189688832 | bytes 37765120 | tf_op jit(solution)/shard_map/hqs,sd->hqd/dot_general | solution.py:81
  236.4 0.0 collective-permute-done.1
  236.5 15.7 %divide_convert_fusion = bf16[512,4,128]{0,2,1:T(8,128)(2,1)S(1)} fusion(f32[512,4,128]{0,2,1:T(8,128)} %fusion.41, bf16[4096,128]{0,1:T(8,128)(2,1)} %collective-permute-done.1, f32[4,512,4096]{2,1,0:T(8,128)} %get-tuple-element.19, f32[4,512]{1,0:T(4,128)S(1)} %get-tuple-element.18, pred[512,4096]{1,0:T(8,128)(4,1)S(1)} %get-tuple-element.14, ...), kind=kOutput, calls=%fused_computation.54 | convolution fusion | flops 2190475264 | bytes 38297600 | tf_op jit(solution)/shard_map/hqs,sd->hqd/dot_general | solution.py:81
  252.2 0.0 copy-start.5
  252.2 0.0 copy-start.6
  252.2 11.6 %multiply_bitcast_fusion = f32[64,64,8,128]{3,2,1,0:T(8,128)} fusion(bf16[512,512]{0,1:T(8,128)(2,1)S(1)} %bitcast.86, bf16[512,8192]{1,0:T(8,128)(2,1)} %param.17, f32[8192]{0:T(1024)S(1)} %add_convert_fusion.2), kind=kOutput, calls=%fused_computation.21 | convolution fusion | flops 4299161600 | bytes 25722880 | tf_op jit(solution)/shard_map/dot_general | solution.py:153
  263.8 0.0 copy-done.5
  263.8 0.0 copy-done.6
  263.8 0.0 copy-start.7
  263.8 21.9 %clamp_convert_fusion = bf16[512,64,128]{0,2,1:T(8,128)(2,1)} fusion(f32[128,128,1]{0,1,2:T(8,128)S(1)} %copy-done.6, f32[64,64,8,128]{3,2,1,0:T(8,128)} %multiply_bitcast_fusion, f32[512,64]{0,1:T(8,128)S(1)} %copy-done.5), kind=kOutput, calls=%fused_computation.20 | convolution fusion | flops 6455033856 | bytes 25362432 | tf_op jit(solution)/shard_map/rbi,ij->rbj/dot_general | solution.py:53
  285.7 0.0 reduce-scatter.2.cloned.1.call-update
  285.8 0.0 all-gather.5.cloned.1.call-start
  285.8 0.0 copy-done.7
  285.9 0.1 copy.34
  286.0 0.1 copy.35
  286.1 0.7 dynamic-slice_convert_fusion
  286.8 0.7 multiply_exponential_fusion.2
  287.6 145.6 %reduce-scatter.2.cloned.1.call-done = bf16[512,1024]{0,1:T(8,128)(2,1)} async-done(((bf16[512,8192]{0,1:T(8,128)(2,1)}), bf16[512,1024]{0,1:T(8,128)(2,1)}) %reduce-scatter.2.cloned.1.call-update) | async-done | bytes 1048592 | tf_op jit(solution)/shard_map/reduce_scatter | solution.py:155
  433.1 4.8 fusion.31
  437.9 1.9 copy.33
  439.8 1.7 fusion.25
  441.5 19.7 %psum.7 = f32[512]{0:T(512)S(1)} all-reduce(f32[512]{0:T(512)S(1)} %get-tuple-element.5), channel_id=1, replica_groups=mesh['groups'=2,'ctx'=2,'tp'=8] {'tp'}, use_global_device_ids=true, to_apply=%region_7.8 | all-reduce | flops 512 | bytes 4096 | tf_op jit(solution)/shard_map/psum | solution.py:166
  461.2 0.6 mul.292
  461.8 1.5 fusion.29
  463.3 0.0 all-gather.5.cloned.1.call-update
  463.4 0.1 copy.37
  463.5 122.1 %all-gather.5.cloned.1.call-done = bf16[512,8192]{1,0:T(8,128)(2,1)} async-done(((bf16[512,1024]{1,0:T(8,128)(2,1)}), bf16[512,8192]{1,0:T(8,128)(2,1)}) %all-gather.5.cloned.1.call-update) | async-done | bytes 8388624 | tf_op jit(solution)/shard_map/all_gather | solution.py:172
  585.6 0.0 copy-start.1
  585.6 4.6 mul.295
  590.2 0.0 copy-done.1
  590.2 12.2 %fusion.9 = bf16[512,8192]{1,0:T(8,128)(2,1)} fusion(f32[64,8,64,128]{3,2,1,0:T(8,128)S(1)} %bitcast.81, bf16[512,8192]{1,0:T(8,128)(2,1)S(1)} %copy-done.1), kind=kLoop, calls=%fused_computation.16 | loop fusion | flops 12582912 | bytes 33554432 | tf_op jit(solution)/shard_map/convert_element_type | solution.py:177
  (10 shorter events, 0.1 us)
Async XLA Ops:
  6.5 130.7 %all-gather.3.cloned.1.call-start = ((), (), s32[]{:S(2)}) async-start(), calls=%async_computation.1 | async-start | bytes 9437184 | tf_op jit(solution)/shard_map/all_gather | solution.py:113
  7.3 425.9 %reduce-scatter.2.cloned.1.call-start = ((), (), s32[]{:S(2)}) async-start(), calls=%async_computation.2 | async-start | bytes 9437184 | tf_op jit(solution)/shard_map/reduce_scatter | solution.py:155
  9.7 178.7 %collective-permute-start = (bf16[4096,128]{1,0:T(8,128)(2,1)}, bf16[4096,128]{1,0:T(8,128)(2,1)}, u32[]{:S(2)}, u32[]{:S(2)}) collective-permute-start(bf16[4096,128]{1,0:T(8,128)(2,1)} %constant_dynamic-slice_fusion.1), channel_id=1, source_target_pairs={{0,8},{8,0},{1,9},{9,1},{2,10},{10,2},{3,11},{11,3},{4,12},{12,4},... | collective-permute-start | bytes 3145736 | tf_op jit(solution)/shard_map/ppermute | solution.py:19
  11.4 142.3 %copy-start.2 = (bf16[4096,128]{1,0:T(8,128)(2,1)}, bf16[4096,128]{1,0:T(8,128)(2,1)S(1)}, u32[]{:S(2)}) copy-start(bf16[4096,128]{1,0:T(8,128)(2,1)S(1)} %constant_dynamic-slice_fusion) | copy-start | bytes 3145732
  12.7 223.7 %collective-permute-start.1 = (bf16[4096,128]{0,1:T(8,128)(2,1)}, bf16[4096,128]{0,1:T(8,128)(2,1)}, u32[]{:S(2)}, u32[]{:S(2)}) collective-permute-start(bf16[4096,128]{0,1:T(8,128)(2,1)} %copy.39), channel_id=1, source_target_pairs={{0,8},{8,0},{1,9},{9,1},{2,10},{10,2},{3,11},{11,3},{4,12},{12,4},... | collective-permute-start | bytes 3145736 | tf_op jit(solution)/shard_map/ppermute | solution.py:19
  15.0 3.3 copy-start.4
  156.7 16.0 %copy-start = (pred[512,4096]{1,0:T(8,128)(4,1)S(1)}, pred[512,4096]{1,0:T(8,128)(4,1)}, u32[]{:S(2)}) copy-start(pred[512,4096]{1,0:T(8,128)(4,1)} %get-tuple-element.15) | copy-start | bytes 6291460
  203.7 15.7 %copy-start.3 = (bf16[4096,128]{1,0:T(8,128)(2,1)S(1)}, bf16[4096,128]{1,0:T(8,128)(2,1)}, u32[]{:S(2)}) copy-start(bf16[4096,128]{1,0:T(8,128)(2,1)} %copy-done.2) | copy-start | bytes 3145732
  252.2 11.6 %copy-start.5 = (f32[512,64]{0,1:T(8,128)S(1)}, f32[512,64]{0,1:T(8,128)}, u32[]{:S(2)}) copy-start(f32[512,64]{0,1:T(8,128)} %exponential_multiply_fusion) | copy-start | bytes 393220
  252.2 11.6 %copy-start.6 = (f32[128,128,1]{0,1,2:T(8,128)S(1)}, f32[128,128,1]{0,1,2:T(8,128)}, u32[]{:S(2)}) copy-start(f32[128,128,1]{0,1,2:T(8,128)} %constant.88) | copy-start | bytes 196612
  263.8 22.0 %copy-start.7 = (s32[16,64]{1,0:T(8,128)S(1)}, s32[16,64]{1,0:T(8,128)}, u32[]{:S(2)}) copy-start(s32[16,64]{1,0:T(8,128)} %param.21) | copy-start | bytes 12292
  285.8 299.9 %all-gather.5.cloned.1.call-start = ((), (), s32[]{:S(2)}) async-start(), calls=%async_computation.3 | async-start | bytes 9437184 | tf_op jit(solution)/shard_map/all_gather | solution.py:172
  585.6 4.6 copy-start.1
Sparse Core Ops, SparseCore 0:
  9.5 127.6 all-gather.2
  285.9 147.1 reduce-scatter.1
  463.5 122.1 all-gather.4
where the time goes:
time: 618 us; the launch traced here: 609 us
  waiting for transfers between devices  384 us (62%)
  matrix products  114 us (18%)
  other arithmetic  62.2 us (10%)
  blocking collectives  19.7 us (3%)
  local copies, waits for them, and re-layouts  14.9 us (2%)
  between operations  14.2 us (2%)
    reduce_scatter x1, waiting for transfers between devices, local(): lax.psum_scatter(codes.astype(jnp.bfloat16), 'tp', scatter_dimension=1, t...  146 us
    all_gather x1, waiting for transfers between devices, local(): whole_code = lax.all_gather(norm_code, 'tp', axis=1, tiled=True)  122 us
    all_gather x1, waiting for transfers between devices, local(): gathered = lax.all_gather(hidden_in, 'tp', axis=1, tiled=True)  115 us
    dot_general x2, matrix products, attend_block(): jnp.einsum('hqs,sd->hqd', weights_f.astype(jnp.bfloat16), value_block, pr...  32.7 us
    reduce_sum x2, other arithmetic, attend_block(): totals = jnp.sum(weights_f, axis=2)  31.4 us
    dot_general x2, matrix products, attend_block(): jnp.einsum('hqd,sd->hqs', queries, key_block, preferred_element_type=jnp....  31.3 us
    dot_general x1, matrix products, encode(): jnp.einsum('rbi,ij->rbj', blocks, hadamard, precision=lax.Precision.HIGHEST)  21.9 us
    psum x1, blocking collectives, local(): squares = lax.psum(jnp.sum(resid_f * resid_f, axis=1), 'tp')  19.7 us
  transfers between devices with their start and end apart: 5, of which 3 were waited for; matrix products, arithmetic and copies ran while one was open for 19% of the time, Pallas kernels for 0%

commit v1 on v0

v1 whole, which is shorter than its diff:
```python
import functools
import math

import jax
import jax.numpy as jnp
from jax import lax
from jax.experimental import pallas as pl
from jax.experimental.pallas import tpu as pltpu
from jax.sharding import PartitionSpec as P

HD = 128
KVH = 4
HB = 128
RB = 32
MIB = 1 << 20
EPS = 1e-05
LOG2E = math.log2(math.e)


def _params(mib, **kw):
    return pltpu.CompilerParams(vmem_limit_bytes=mib * MIB, **kw)


def _permute(value, axis, pairs):
    return lax.ppermute(value, axis, pairs)


def _both(value, axis, count):
    if count == 2:
        other = _permute(value, axis, [(0, 1), (1, 0)])
        first = lax.axis_index(axis) == 0
        return jnp.stack([jnp.where(first, value, other), jnp.where(first, other, value)])
    return lax.all_gather(value, axis, axis=0)


def _gather_line(value, zc, yc):
    n = zc * yc
    z = lax.axis_index("tp") // yc
    y = lax.axis_index("tp") % yc
    bar = lax.optimization_barrier

    def across(v):
        return _permute(v, "tp", [(s, s ^ 1) for s in range(n)])

    def up(v, k):
        return _permute(v, "tp", [(s, s + yc) for s in range(n) if k - 1 <= s // yc < zc - 1])

    def down(v, k):
        return _permute(v, "tp", [(s, s - yc) for s in range(n) if 1 <= s // yc <= zc - k])

    def stream(x):
        y0, u1, d1 = bar((across(x), up(x, 1), down(x, 1)))
        va = jnp.where(z == 0, d1, u1)
        ya, u2, d2 = bar((across(va), up(u1, 2), down(d1, 2)))
        vb = jnp.where(z == 0, d2, jnp.where(z == 3, u2, d1))
        yb, u3, d3 = bar((across(vb), up(u2, 3), down(d2, 3)))
        vc = jnp.where(z == 0, d3, jnp.where(z == 1, d2, jnp.where(z == 2, u2, u3)))
        return [x, va, vb, vc, y0, ya, yb, across(vc)]

    def pick(a, b, c, d):
        return jnp.where(z == 0, a, jnp.where(z == 1, b, jnp.where(z == 2, c, d)))

    layers = [z, pick(1, 0, 1, 2), pick(2, 2, 3, 1), pick(3, 3, 0, 0)]
    ids = [l * yc + y for l in layers] + [l * yc + (1 - y) for l in layers]
    half = value.shape[1] // 2
    left = stream(value[:, :half])
    right = stream(value[:, half:])
    return left, right, jnp.stack(ids).astype(jnp.int32)


def gather_tp(value, zc, yc):
    if zc == 4 and yc == 2:
        return _gather_line(value, zc, yc)
    n = zc * yc
    whole = lax.all_gather(value, "tp", axis=0)
    half = value.shape[1] // 2
    left = [whole[i, :, :half] for i in range(n)]
    right = [whole[i, :, half:] for i in range(n)]
    return left, right, jnp.arange(n, dtype=jnp.int32)


def _query_kernel(n, heads, ids, *refs):
    parts = refs[: 2 * n]
    gain, weight, cos, sin, out = refs[2 * n :]
    half = parts[0].shape[1]
    d = 2 * n * half
    total = None
    for p in parts:
        f = p[...].astype(jnp.float32)
        s = jnp.sum(f * f, axis=1, keepdims=True)
        total = s if total is None else total + s
    r = lax.rsqrt(total / d + EPS)
    acc = None
    for i in range(2 * n):
        side, slot = i // n, i % n
        at = ids[slot]
        f = parts[i][...].astype(jnp.float32)
        normed = (f * r * gain[2 * at + side]).astype(jnp.bfloat16)
        rows = pl.ds(pl.multiple_of(at * (2 * half) + side * half, half), half)
        t = jnp.dot(normed, weight[rows, :], preferred_element_type=jnp.float32)
        acc = t if acc is None else acc + t
    for h in range(heads):
        v = acc[:, h * HD : (h + 1) * HD]
        turned = v * cos[...] + pltpu.roll(v, HD // 2, 1) * sin[...]
        out[h] = turned.astype(jnp.bfloat16)


def project_queries(left, right, ids, gain, weight, cos, sin):
    n = len(left)
    rows, half = left[0].shape
    d, width = weight.shape
    heads = width // HD
    tile = 128
    gains = gain.astype(jnp.float32).reshape(2 * n, 1, half)
    grid_spec = pltpu.PrefetchScalarGridSpec(
        num_scalar_prefetch=1,
        grid=(rows // tile,),
        in_specs=[pl.BlockSpec((tile, half), lambda i, ids: (i, 0))] * (2 * n)
        + [
            pl.BlockSpec((2 * n, 1, half), lambda i, ids: (0, 0, 0)),
            pl.BlockSpec((d, width), lambda i, ids: (0, 0), pipeline_mode=pl.Buffered(1)),
            pl.BlockSpec((tile, HD), lambda i, ids: (i, 0)),
            pl.BlockSpec((tile, HD), lambda i, ids: (i, 0)),
        ],
        out_specs=pl.BlockSpec((heads, tile, HD), lambda i, ids: (0, i, 0)),
    )
    return pl.pallas_call(
        functools.partial(_query_kernel, n, heads),
        grid_spec=grid_spec,
        out_shape=jax.ShapeDtypeStruct((heads, rows, HD), jnp.bfloat16),
        compiler_params=_params(48),
        cost_estimate=pl.CostEstimate(
            flops=2 * rows * d * width, bytes_accessed=2 * (rows * d + d * width), transcendentals=0
        ),
        name="query_projection",
    )(ids, *left, *right, gains, weight, cos, sin)


CK = 512


def _attend_kernel(heads, tile, span, info, q_ref, k_ref, v_ref, out, s_ref, m_ref, l_ref, acc_ref):
    step = pl.program_id(0)
    scale = LOG2E / math.sqrt(HD)
    m = heads * tile
    q = q_ref[...].reshape(m, HD)
    first_pos = info[0] + step * tile
    row_pos = first_pos + lax.rem(lax.broadcasted_iota(jnp.int32, (m, CK), 0), tile)

    def scores(base, j, masked):
        keys = k_ref[pl.ds(pl.multiple_of(base + j * CK, CK), CK), :]
        s = lax.dot_general(q, keys, (((1,), (1,)), ((), ())), preferred_element_type=jnp.float32)
        if masked:
            col = base + j * CK + lax.broadcasted_iota(jnp.int32, (m, CK), 1)
            s = jnp.where(col <= row_pos, s, -1e30)
        s_ref[:, pl.ds(pl.multiple_of(j * CK, CK), CK)] = s
        top = m_ref[...]
        for c in range(CK // 128):
            top = jnp.maximum(top, s[:, c * 128 : (c + 1) * 128])
        m_ref[...] = top

    def weigh(base, j, top):
        s = s_ref[:, pl.ds(pl.multiple_of(j * CK, CK), CK)]
        p = jnp.exp2((s - top) * scale)
        total = l_ref[...]
        for c in range(CK // 128):
            total = total + p[:, c * 128 : (c + 1) * 128]
        l_ref[...] = total
        vals = v_ref[pl.ds(pl.multiple_of(base + j * CK, CK), CK), :]
        acc_ref[...] += jnp.dot(p.astype(jnp.bfloat16), vals, preferred_element_type=jnp.float32)

    def block(base, full, count):
        m_ref[...] = jnp.full(m_ref.shape, -1e30, jnp.float32)
        l_ref[...] = jnp.zeros(l_ref.shape, jnp.float32)
        acc_ref[...] = jnp.zeros(acc_ref.shape, jnp.float32)

        def loop(n, f):
            if isinstance(n, int):
                for j in range(n):
                    f(j)
            else:
                lax.fori_loop(0, n, lambda j, c: (f(j), c)[1], 0)

        loop(full, lambda j: scores(base, j, False))
        if count is not full:
            lax.fori_loop(full, count, lambda j, c: (scores(base, j, True), c)[1], 0)
        top = jnp.max(m_ref[...], axis=1, keepdims=True)
        loop(count, lambda j: weigh(base, j, top))
        return top, jnp.sum(l_ref[...], axis=1, keepdims=True), acc_ref[...]

    chunks = span // CK
    blocks = k_ref.shape[0] // span
    top, total, acc = block(0, chunks, chunks)
    for b in range(1, blocks):
        base = b * span
        full = jnp.clip((first_pos + 1 - base) // CK, 0, chunks)
        count = jnp.clip((first_pos + tile - 1 - base) // CK + 1, 0, chunks)
        top2, total2, acc2 = block(base, full, count)
        new = jnp.maximum(top, top2)
        f1 = jnp.exp2((top - new) * scale)
        f2 = jnp.exp2((top2 - new) * scale)
        acc = f1 * acc + f2 * acc2
        total = f1 * total + f2 * total2
        top = new
    res = (acc / total).astype(jnp.bfloat16)
    for h in range(heads):
        out[:, h * HD : (h + 1) * HD] = res[h * tile : (h + 1) * tile]


def attend(q, keys, values, start, span):
    heads, rows, _ = q.shape
    tile = min(512 // heads, rows)
    m = heads * tile
    total = keys.shape[0]
    grid_spec = pltpu.PrefetchScalarGridSpec(
        num_scalar_prefetch=1,
        grid=(rows // tile,),
        in_specs=[
            pl.BlockSpec((heads, tile, HD), lambda i, info: (0, i, 0)),
            pl.BlockSpec((total, HD), lambda i, info: (0, 0), pipeline_mode=pl.Buffered(1)),
            pl.BlockSpec((total, HD), lambda i, info: (0, 0), pipeline_mode=pl.Buffered(1)),
        ],
        out_specs=pl.BlockSpec((tile, heads * HD), lambda i, info: (i, 0)),
        scratch_shapes=[
            pltpu.VMEM((m, span), jnp.float32),
            pltpu.VMEM((m, 128), jnp.float32),
            pltpu.VMEM((m, 128), jnp.float32),
            pltpu.VMEM((m, HD), jnp.float32),
        ],
    )
    return pl.pallas_call(
        functools.partial(_attend_kernel, heads, tile, span),
        grid_spec=grid_spec,
        out_shape=jax.ShapeDtypeStruct((rows, heads * HD), jnp.bfloat16),
        compiler_params=_params(48),
        cost_estimate=pl.CostEstimate(
            flops=4 * heads * rows * total * HD, bytes_accessed=4 * total * HD, transcendentals=heads * rows * total
        ),
        name="attend",
    )(start, q, keys, values)


def _spin(x, table):
    hi = x.astype(jnp.bfloat16)
    lo = (x - hi.astype(jnp.float32)).astype(jnp.bfloat16)
    return jnp.dot(hi, table, preferred_element_type=jnp.float32) + jnp.dot(
        lo, table, preferred_element_type=jnp.float32
    )


def _by_row_block(x, scale):
    blocks = scale.shape[0]
    rows, cols = x.shape
    return (x.reshape(blocks, rows // blocks, cols) * scale[:, None, :]).reshape(rows, cols)


def _code_kernel(zc, info, *refs):
    atts = refs[:zc]
    own, far, table, sign, scale, out = refs[zc:]
    spin = table[...] * sign[...]
    csz, gsz = far.shape[0], far.shape[1]
    total = None
    for k in range(zc):
        if k == 0:
            w = own[...]
        else:
            w = jnp.concatenate([far[c, g, k - 1] for g in range(gsz) for c in range(csz)], axis=0)
        part = jnp.dot(atts[k][...], w, preferred_element_type=jnp.float32)
        spun = _spin(part, spin)
        coded = jnp.clip(_by_row_block(spun, scale[...]), -127.0, 127.0)
        coded = coded.astype(jnp.bfloat16).astype(jnp.float32)
        total = coded if total is None else total + coded
    out[...] = total.astype(out.dtype)


def code_terms(atts, own, far, table, signs, scale, z, side, out_type):
    zc = len(atts)
    rows, depth = atts[0].shape
    csz, gsz, _, piece, cols = far.shape
    width = cols // 2
    tile = table.shape[0]
    steps = width // tile
    info = jnp.stack([z * (cols // tile) + side * steps, side * steps]).astype(jnp.int32)
    grid_spec = pltpu.PrefetchScalarGridSpec(
        num_scalar_prefetch=1,
        grid=(steps,),
        in_specs=[pl.BlockSpec((rows, depth), lambda j, info: (0, 0), pipeline_mode=pl.Buffered(1))] * zc
        + [
            pl.BlockSpec((depth, tile), lambda j, info: (0, info[0] + j)),
            pl.BlockSpec((csz, gsz, zc - 1, piece, tile), lambda j, info: (0, 0, 0, 0, info[1] + j)),
            pl.BlockSpec((tile, tile), lambda j, info: (0, 0)),
            pl.BlockSpec((tile, 1), lambda j, info: (j, 0)),
            pl.BlockSpec((scale.shape[0], tile), lambda j, info: (0, j)),
        ],
        out_specs=pl.BlockSpec((rows, tile), lambda j, info: (0, j)),
    )
    return pl.pallas_call(
        functools.partial(_code_kernel, zc),
        grid_spec=grid_spec,
        out_shape=jax.ShapeDtypeStruct((rows, width), out_type),
        compiler_params=_params(48),
        cost_estimate=pl.CostEstimate(
            flops=2 * zc * rows * width * (depth + 2 * tile), bytes_accessed=2 * zc * depth * width, transcendentals=0
        ),
        name="code_terms",
    )(info, *atts, own, far, table, signs, scale)


def _residual_kernel(mine, theirs, hidden, table, scale, sign, out):
    summed = mine[...] + theirs[...].astype(jnp.float32)
    tile = table.shape[0]
    for j in range(summed.shape[1] // tile):
        at = slice(j * tile, (j + 1) * tile)
        spun = _spin(summed[:, at], table[...])
        projected = _by_row_block(spun, scale[:, at]) * sign[:, at]
        out[:, at] = (hidden[:, at].astype(jnp.float32) + projected).astype(jnp.bfloat16)


def add_residual(mine, theirs, hidden, table, scale, sign):
    rows, width = mine.shape
    tile = min(256, rows)
    blocks = scale.shape[0] * tile // rows
    return pl.pallas_call(
        _residual_kernel,
        grid=(rows // tile,),
        in_specs=[
            pl.BlockSpec((tile, width), lambda i: (i, 0)),
            pl.BlockSpec((tile, width), lambda i: (i, 0)),
            pl.BlockSpec((tile, width), lambda i: (i, 0)),
            pl.BlockSpec(table.shape, lambda i: (0, 0)),
            pl.BlockSpec((blocks, width), lambda i: (i, 0)),
            pl.BlockSpec((1, width), lambda i: (0, 0)),
        ],
        out_specs=pl.BlockSpec((tile, width), lambda i: (i, 0)),
        out_shape=jax.ShapeDtypeStruct((rows, width), jnp.bfloat16),
        compiler_params=_params(40),
        cost_estimate=pl.CostEstimate(
            flops=4 * rows * width * table.shape[0], bytes_accessed=10 * rows * width, transcendentals=0
        ),
        name="residual",
    )(mine, theirs, hidden, table, scale, sign)


def _norm_kernel(n, ids, *refs):
    parts = refs[: 2 * n]
    gain, down, up, out = refs[2 * n :]
    rows, half = parts[0].shape
    d = 2 * n * half
    total = None
    for p in parts:
        f = p[...].astype(jnp.float32)
        s = jnp.sum(f * f, axis=1, keepdims=True)
        total = s if total is None else total + s
    r = lax.rsqrt(total / d + EPS)
    for i in range(2 * n):
        side, slot = i // n, i % n
        at = 2 * ids[slot] + side
        scaled = parts[i][...].astype(jnp.float32) * r * gain[at]
        code = jnp.clip(_by_row_block(scaled, down[0, at]), -127.0, 127.0).astype(jnp.bfloat16)
        value = _by_row_block(code.astype(jnp.float32), up[0, at]).astype(jnp.bfloat16)
        out[:, pl.ds(pl.multiple_of(at * half, half), half)] = value


def norm_rows(left, right, ids, gain, exps):
    n = len(left)
    rows, half = left[0].shape
    d = 2 * n * half
    tile = 128
    steps = rows // tile
    blocks = tile // RB
    gains = gain.astype(jnp.float32).reshape(2 * n, 1, half)
    e = jnp.repeat(exps.astype(jnp.float32), HB, axis=1).reshape(steps, blocks, 2 * n, half).transpose(0, 2, 1, 3)
    grid_spec = pltpu.PrefetchScalarGridSpec(
        num_scalar_prefetch=1,
        grid=(steps,),
        in_specs=[pl.BlockSpec((tile, half), lambda i, ids: (i, 0))] * (2 * n)
        + [
            pl.BlockSpec((2 * n, 1, half), lambda i, ids: (0, 0, 0)),
            pl.BlockSpec((1, 2 * n, blocks, half), lambda i, ids: (i, 0, 0, 0)),
            pl.BlockSpec((1, 2 * n, blocks, half), lambda i, ids: (i, 0, 0, 0)),
        ],
        out_specs=pl.BlockSpec((tile, d), lambda i, ids: (i, 0)),
    )
    return pl.pallas_call(
        functools.partial(_norm_kernel, n),
        grid_spec=grid_spec,
        out_shape=jax.ShapeDtypeStruct((rows, d), jnp.bfloat16),
        compiler_params=_params(40),
        cost_estimate=pl.CostEstimate(flops=8 * rows * d, bytes_accessed=4 * rows * d, transcendentals=0),
        name="norm",
    )(ids, *left, *right, gains, jnp.exp2(-e), jnp.exp2(e))


def hadamard_table(order):
    table = jnp.ones((1, 1), dtype=jnp.float32)
    while table.shape[0] < order:
        upper = jnp.concatenate([table, table], axis=1)
        lower = jnp.concatenate([table, -table], axis=1)
        table = jnp.concatenate([upper, lower], axis=0)
    return table


def rotary_tables(positions):
    half = HD // 2
    inv_freq = jnp.exp(-(jnp.arange(half, dtype=jnp.float32) * (2.0 / HD)) * math.log(500000.0))
    angles = positions.astype(jnp.float32)[:, None] * inv_freq[None, :]
    cos, sin = jnp.cos(angles), jnp.sin(angles)
    return jnp.concatenate([cos, cos], axis=1), jnp.concatenate([-sin, sin], axis=1)


def local(
    hidden_in,
    attn_gain,
    query_weight,
    keys,
    values,
    offset,
    out_weight,
    sign_bits,
    attn_exps,
    norm_gain,
    norm_exps,
):
    n_tp, csz, gsz = lax.axis_size("tp"), lax.axis_size("ctx"), lax.axis_size("groups")
    yc = 2 if n_tp % 2 == 0 else 1
    zc = n_tp // yc
    tp, ctx, grp = lax.axis_index("tp"), lax.axis_index("ctx"), lax.axis_index("groups")
    z, y = tp // yc, tp % yc
    rows, width = hidden_in.shape
    d = width * n_tp
    heads = query_weight.shape[1] // HD
    all_heads = heads * n_tp
    depth = out_weight.shape[0]
    cols = d // zc

    column = tp * heads // (all_heads // KVH) * HD
    own_keys = lax.dynamic_slice_in_dim(keys, column, HD, 1)
    own_values = lax.dynamic_slice_in_dim(values, column, HD, 1)
    span = keys.shape[0]
    all_keys = _both(own_keys, "ctx", csz).reshape(csz * span, HD)
    all_values = _both(own_values, "ctx", csz).reshape(csz * span, HD)

    left, right, ids = gather_tp(hidden_in, zc, yc)
    start = (offset[0] + ctx * rows).astype(jnp.int32)
    cos, sin = rotary_tables(start + jnp.arange(rows, dtype=jnp.int32))
    q = project_queries(left, right, ids, attn_gain, query_weight, cos, sin)

    piece = depth // (gsz * csz)
    mine = lax.dynamic_slice_in_dim(out_weight, (grp * csz + ctx) * piece, piece, 0)
    far = []
    for k in range(1, zc):
        block = lax.dynamic_slice_in_dim(mine, (z + k) % zc * cols, cols, 1)
        far.append(_permute(block, "tp", [(s, (s + k * yc) % n_tp) for s in range(n_tp)]))
    far = _both(_both(jnp.stack(far), "groups", gsz), "ctx", csz)

    attended = attend(q, all_keys, all_values, start.reshape(1), span)
    atts = [attended] + [
        _permute(attended, "tp", [(s, (s + k * yc) % n_tp) for s in range(n_tp)]) for k in range(1, zc)
    ]

    tile = 2 * HB
    h = hadamard_table(HB)
    zero = jnp.zeros_like(h)
    table = jnp.concatenate([jnp.concatenate([h, zero], 1), jnp.concatenate([zero, h], 1)], 0).astype(jnp.bfloat16)
    signs = (2 * sign_bits - 1).astype(jnp.bfloat16)
    root = 1.0 / math.sqrt(HB)

    def columns_of(side):
        return (z * yc + side) * width

    def code_half(side, out_type):
        e = lax.dynamic_slice_in_dim(attn_exps, columns_of(side) // HB, width // HB, 1).astype(jnp.float32)
        scale = jnp.repeat(jnp.exp2(-e) * root, HB, axis=1)
        sg = lax.dynamic_slice_in_dim(signs, columns_of(side), width, 0)[:, None]
        return code_terms(atts, out_weight, far, table, sg, scale, z, side, out_type)

    sent = code_half(1 - y, jnp.bfloat16)
    theirs = _permute(sent, "tp", [(s, s ^ 1) for s in range(n_tp)])
    mine_sum = code_half(y, jnp.float32)
    e = lax.dynamic_slice_in_dim(attn_exps, columns_of(y) // HB, width // HB, 1).astype(jnp.float32)
    up = jnp.repeat(jnp.exp2(e) * root, HB, axis=1)
    sg = lax.dynamic_slice_in_dim(signs, columns_of(y), width, 0).astype(jnp.float32)[None, :]
    residual = add_residual(mine_sum, theirs, hidden_in, table, up, sg)

    left, right, ids = gather_tp(residual, zc, yc)
    return norm_rows(left, right, ids, norm_gain, norm_exps)


def solution(mesh):
    return jax.shard_map(
        local,
        mesh=mesh,
        in_specs=(
            P(("groups", "ctx"), "tp"),
            P(),
            P(None, "tp"),
            P(("groups", "ctx"), None),
            P(("groups", "ctx"), None),
            P("groups"),
            P("tp", None),
            P(),
            P(("groups", "ctx"), None),
            P(),
            P(("groups", "ctx"), None),
        ),
        out_specs=P(("groups", "ctx"), None),
        check_vma=False,
    )
```

time: 618 us -> 411 us (0.67); the launches traced: 609 us -> 411 us
  waiting for transfers between devices: 384 us -> 206 us
  matrix products: 114 us -> 0 us
  starting transfers between devices: 0.59 us -> 78.6 us
  Pallas kernels: 0 us -> 74.3 us
  other arithmetic: 62.2 us -> 27.3 us
  blocking collectives: 19.7 us -> 0 us
  between operations: 14.2 us -> 1.27 us
  local copies, waits for them, and re-layouts: 14.9 us -> 23.2 us
    all_gather x2 -> x0, waiting for transfers between devices: 238 us -> none  [the longest x1 122 us: local(): whole_code = lax.all_gather(norm_code, 'tp', axis=1, tiled=True)]
    ppermute x2 -> x51, waiting for transfers between devices: 0.01 us -> 206 us  [_permute(): return lax.ppermute(value, axis, pairs)]
    reduce_scatter x1 -> x0, waiting for transfers between devices: 146 us -> none  [local(): lax.psum_scatter(codes.astype(jnp.bfloat16), 'tp', scatter_dimension=1, t...]
    dot_general x8 -> x0, matrix products: 114 us -> none  [the longest x2 32.7 us: attend_block(): jnp.einsum('hqs,sd->hqd', weights_f.astype(jnp.bfloat16), value_block, pr...]
    ppermute x2 -> x51, starting transfers between devices: 0.51 us -> 78.6 us  [_permute(): return lax.ppermute(value, axis, pairs)]
    pallas_call x0 -> x6, Pallas kernels: none -> 74.3 us  [the longest x1 31.3 us: attend(): pl.pallas_call(functools.partial(_attend_kernel, heads, tile, span), grid...]
    reduce_sum x4 -> x0, other arithmetic: 38.1 us -> none  [the longest x2 31.4 us: attend_block(): totals = jnp.sum(weights_f, axis=2)]
    psum x1 -> x0, blocking collectives: 19.7 us -> none  [local(): squares = lax.psum(jnp.sum(resid_f * resid_f, axis=1), 'tp')]
  transfers between devices with their start and end apart: 5 -> 51, of which waited for: 3 -> 29; matrix products, arithmetic and copies ran while one was open for 19% -> 11% of each run, Pallas kernels for 0% -> 12%
where the time goes in v1:
time: 411 us
  waiting for transfers between devices  206 us (50%)
  starting transfers between devices  78.6 us (19%)
  Pallas kernels  74.3 us (18%)
  other arithmetic  27.3 us (7%)
  local copies, waits for them, and re-layouts  23.2 us (6%)
    ppermute x51, waiting for transfers between devices, _permute(): return lax.ppermute(value, axis, pairs)  206 us
    ppermute x51, starting transfers between devices, _permute(): return lax.ppermute(value, axis, pairs)  78.6 us
    pallas_call x1, Pallas kernels, attend(): pl.pallas_call(functools.partial(_attend_kernel, heads, tile, span), grid...  31.3 us
    pallas_call x2, Pallas kernels, code_terms(): pl.pallas_call(functools.partial(_code_kernel, zc), grid_spec=grid_spec,...  16.9 us
    another operation x8, other arithmetic, _both(): jnp.stack([jnp.where(first, value, other), jnp.where(first, other, value)])  13.4 us
    pallas_call x1, Pallas kernels, norm_rows(): pl.pallas_call(functools.partial(_norm_kernel, n), grid_spec=grid_spec, o...  13.2 us
    pallas_call x1, Pallas kernels, project_queries(): pl.pallas_call(functools.partial(_query_kernel, n, heads), grid_spec=grid...  11.9 us
  transfers between devices with their start and end apart: 51, of which 29 were waited for; matrix products, arithmetic and copies ran while one was open for 11% of the time, Pallas kernels for 12%

profile of v1, /device:TPU:0, one launch (start us, length us, event | category | flops | bytes accessed | tf_op | source)
XLA Modules:
  0.0 410.9 jit_solution(10068987058864742969)
XLA Ops:
  2.6 6.4 %collective-permute-start.11 = (bf16[512,512]{1,0:T(8,128)(2,1)S(1)}, bf16[512,512]{1,0:T(8,128)(2,1)}, u32[]{:S(2)}, u32[]{:S(2)}) collective-permute-start(bf16[512,512]{1,0:T(8,128)(2,1)S(1)} %get-tuple-element.92.refs_8_), channel_id=1, source_target_pairs={{0,2},{1,3},{2,4},{3,5},{4,6},{5,7},{8,10},{9,11},{10,12},{11,13},... | collective-permute-start | bytes 1572872 | tf_op jit(solution)/shard_map/ppermute | solution.py:25
  8.9 2.0 collective-permute-start.10
  12.2 5.4 %collective-permute-start.1 = (bf16[512,512]{1,0:T(8,128)(2,1)S(1)}, bf16[512,512]{1,0:T(8,128)(2,1)}, u32[]{:S(2)}, u32[]{:S(2)}) collective-permute-start(bf16[512,512]{1,0:T(8,128)(2,1)S(1)} %get-tuple-element.93.refs_0_), channel_id=1, source_target_pairs={{0,2},{1,3},{2,4},{3,5},{4,6},{5,7},{8,10},{9,11},{10,12},{11,13},... | collective-permute-start | bytes 1572872 | tf_op jit(solution)/shard_map/ppermute | solution.py:25
  17.6 2.3 constant_dynamic-slice_fusion.1
  19.9 2.3 constant_dynamic-slice_fusion
  23.7 3.5 fusion.2
  28.0 3.0 collective-permute-start.27
  33.4 1.5 collective-permute-start.14
  36.5 1.8 fusion
  38.3 5.8 %collective-permute-done.25 = bf16[128,2048]{1,0:T(8,128)(2,1)} collective-permute-done((bf16[128,2048]{1,0:T(8,128)(2,1)}, bf16[128,2048]{1,0:T(8,128)(2,1)}, u32[]{:S(2)}, u32[]{:S(2)}) %collective-permute-start.25) | collective-permute-done | bytes 524320 | tf_op jit(solution)/shard_map/ppermute | solution.py:25
  44.1 10.2 %collective-permute-done.27 = bf16[128,2048]{1,0:T(8,128)(2,1)} collective-permute-done((bf16[128,2048]{1,0:T(8,128)(2,1)}, bf16[128,2048]{1,0:T(8,128)(2,1)}, u32[]{:S(2)}, u32[]{:S(2)}) %collective-permute-start.27) | collective-permute-done | bytes 524320 | tf_op jit(solution)/shard_map/ppermute | solution.py:25
  56.7 20.1 %collective-permute-done.26 = bf16[128,2048]{1,0:T(8,128)(2,1)} collective-permute-done((bf16[128,2048]{1,0:T(8,128)(2,1)}, bf16[128,2048]{1,0:T(8,128)(2,1)}, u32[]{:S(2)}, u32[]{:S(2)}) %collective-permute-start.26) | collective-permute-done | bytes 524320 | tf_op jit(solution)/shard_map/ppermute | solution.py:25
  79.6 1.6 collective-permute-start.3
  82.5 2.7 pad_maximum_fusion.4
  85.2 1.8 collective-permute-done.15
  86.9 1.5 collective-permute-start.28
  89.5 1.9 collective-permute-done.3.refs_5_
  92.7 5.4 %collective-permute-done.5 = bf16[512,512]{1,0:T(8,128)(2,1)} collective-permute-done((bf16[512,512]{1,0:T(8,128)(2,1)}, bf16[512,512]{1,0:T(8,128)(2,1)}, u32[]{:S(2)}, u32[]{:S(2)}) %collective-permute-start.5) | collective-permute-done | bytes 524320 | tf_op jit(solution)/shard_map/ppermute | solution.py:25
  101.4 2.0 select_bitcast_fusion.5
  104.7 18.9 %collective-permute-done.28 = bf16[3,128,2048]{2,1,0:T(8,128)(2,1)} collective-permute-done((bf16[3,128,2048]{2,1,0:T(8,128)(2,1)}, bf16[3,128,2048]{2,1,0:T(8,128)(2,1)}, u32[]{:S(2)}, u32[]{:S(2)}) %collective-permute-start.28) | collective-permute-done | bytes 1572896 | tf_op jit(solution)/shard_map/ppermute | solution.py:25
  123.6 1.5 collective-permute-start.16
  125.2 2.1 select_bitcast_fusion.3
  127.2 1.9 pad_maximum_fusion.1
  130.1 6.7 %collective-permute-done.16.refs_14_ = bf16[512,512]{1,0:T(8,128)(2,1)S(1)} collective-permute-done((bf16[512,512]{1,0:T(8,128)(2,1)S(1)}, bf16[512,512]{1,0:T(8,128)(2,1)S(1)}, u32[]{:S(2)}, u32[]{:S(2)}) %collective-permute-start.16) | collective-permute-done | bytes 524320 | tf_op jit(solution)/shard_map/ppermute | solution.py:25
  136.7 1.5 collective-permute-start.6
  138.2 1.6 select_bitcast_fusion.7
  140.7 10.9 %collective-permute-done.6.refs_6_ = bf16[512,512]{1,0:T(8,128)(2,1)S(1)} collective-permute-done((bf16[512,512]{1,0:T(8,128)(2,1)S(1)}, bf16[512,512]{1,0:T(8,128)(2,1)S(1)}, u32[]{:S(2)}, u32[]{:S(2)}) %collective-permute-start.6) | collective-permute-done | bytes 524320 | tf_op jit(solution)/shard_map/ppermute | solution.py:25
  151.8 1.6 collective-permute-start.9
  153.8 9.0 %collective-permute-done.19.refs_15_ = bf16[512,512]{1,0:T(8,128)(2,1)S(1)} collective-permute-done((bf16[512,512]{1,0:T(8,128)(2,1)S(1)}, bf16[512,512]{1,0:T(8,128)(2,1)S(1)}, u32[]{:S(2)}, u32[]{:S(2)}) %collective-permute-start.19) | collective-permute-done | bytes 524320 | tf_op jit(solution)/shard_map/ppermute | solution.py:25
  162.8 8.5 %collective-permute-done.9.refs_7_ = bf16[512,512]{1,0:T(8,128)(2,1)S(1)} collective-permute-done((bf16[512,512]{1,0:T(8,128)(2,1)S(1)}, bf16[512,512]{1,0:T(8,128)(2,1)S(1)}, u32[]{:S(2)}, u32[]{:S(2)}) %collective-permute-start.9) | collective-permute-done | bytes 524320 | tf_op jit(solution)/shard_map/ppermute | solution.py:25
  171.3 11.9 %query_projection.1.q_ref = bf16[4,512,128]{2,1,0:T(8,128)(2,1)S(1)} custom-call(s32[8]{0:T(128)S(1)} %stack.110.ids, bf16[512,512]{1,0:T(8,128)(2,1)S(1)} %get-tuple-element.93.refs_0_, bf16[512,512]{1,0:T(8,128)(2,1)S(1)} %broadcast_select_fusion.3.refs_1_, bf16[512,512]{1,0:T(8,128)(2,1)S(1)} %select_select_fusion.7.refs_2_, ...), custom_call_target="tpu_custom_call" | custom-call | flops 4294967296 | bytes 16777216 | tf_op jit(solution)/shard_map/query_projection/pallas_call | solution.py:127
  183.2 31.3 %attend.1.refs_0_ = bf16[512,512]{1,0:T(8,128)(2,1)S(1)} custom-call(s32[1]{0:T(128)} %bitcast.11.info, bf16[4,512,128]{2,1,0:T(8,128)(2,1)S(1)} %query_projection.1.q_ref, bf16[8192,128]{1,0:T(8,128)(2,1)S(1)} %bitcast.56, bf16[8192,128]{1,0:T(8,128)(2,1)S(1)} %bitcast.55), custom_call_target="tpu_custom_call" | custom-call | flops 8589934592 | bytes 4194304 | tf_op jit(solution)/shard_map/attend/pallas_call | solution.py:231
  214.6 3.5 collective-permute-start.23
  218.1 1.9 collective-permute-start.22
  220.0 2.1 select_bitcast_fusion.1
  222.2 3.2 pad_maximum_fusion.refs_5_
  225.4 2.9 collective-permute-done.24.refs_3_
  228.4 35.6 %collective-permute-done.23.refs_2_ = bf16[512,512]{1,0:T(8,128)(2,1)S(1)} collective-permute-done((bf16[512,512]{1,0:T(8,128)(2,1)S(1)}, bf16[512,512]{1,0:T(8,128)(2,1)S(1)}, u32[]{:S(2)}, u32[]{:S(2)}) %collective-permute-start.23) | collective-permute-done | bytes 524320 | tf_op jit(solution)/shard_map/ppermute | solution.py:25
  264.0 8.8 %code_terms.3 = bf16[512,1024]{1,0:T(8,128)(2,1)} custom-call(s32[2]{0:T(128)S(1)} %pad_add_fusion.1.info, bf16[512,512]{1,0:T(8,128)(2,1)S(1)} %attend.1.refs_0_, bf16[512,512]{1,0:T(8,128)(2,1)S(1)} %collective-permute-done.22.refs_1_, bf16[512,512]{1,0:T(8,128)(2,1)S(1)} %collective-permute-done.23.refs_2_, ...), custom_call_target="tpu_custom_call" | custom-call | flops 4294967296 | bytes 4194304 | tf_op jit(solution)/shard_map/code_terms/pallas_call | solution.py:297
  273.9 8.1 %code_terms.2.mine = f32[512,1024]{1,0:T(8,128)S(1)} custom-call(s32[2]{0:T(128)S(1)} %pad_add_fusion.info, bf16[512,512]{1,0:T(8,128)(2,1)S(1)} %attend.1.refs_0_, bf16[512,512]{1,0:T(8,128)(2,1)S(1)} %collective-permute-done.22.refs_1_, bf16[512,512]{1,0:T(8,128)(2,1)S(1)} %collective-permute-done.23.refs_2_, ...), custom_call_target="tpu_custom_call" | custom-call | flops 4294967296 | bytes 4194304 | tf_op jit(solution)/shard_map/code_terms/pallas_call | solution.py:297
  282.1 15.6 %collective-permute-done.30.theirs = bf16[512,1024]{1,0:T(8,128)(2,1)S(1)} collective-permute-done((bf16[512,1024]{1,0:T(8,128)(2,1)}, bf16[512,1024]{1,0:T(8,128)(2,1)S(1)}, u32[]{:S(2)}, u32[]{:S(2)}) %collective-permute-start.30) | collective-permute-done | bytes 1048608 | tf_op jit(solution)/shard_map/ppermute | solution.py:25
  300.1 4.6 %collective-permute-start.42 = (bf16[512,512]{1,0:T(8,128)(2,1)S(1)}, bf16[512,512]{1,0:T(8,128)(2,1)S(1)}, u32[]{:S(2)}, u32[]{:S(2)}) collective-permute-start(bf16[512,512]{1,0:T(8,128)(2,1)S(1)} %get-tuple-element.90.refs_8_), channel_id=1, source_target_pairs={{0,2},{1,3},{2,4},{3,5},{4,6},{5,7},{8,10},{9,11},{10,12},{11,13},... | collective-permute-start | bytes 1572872 | tf_op jit(solution)/shard_map/ppermute | solution.py:25
  307.3 4.6 %collective-permute-start.32 = (bf16[512,512]{1,0:T(8,128)(2,1)S(1)}, bf16[512,512]{1,0:T(8,128)(2,1)S(1)}, u32[]{:S(2)}, u32[]{:S(2)}) collective-permute-start(bf16[512,512]{1,0:T(8,128)(2,1)S(1)} %get-tuple-element.91.refs_0_), channel_id=1, source_target_pairs={{0,2},{1,3},{2,4},{3,5},{4,6},{5,7},{8,10},{9,11},{10,12},{11,13},... | collective-permute-start | bytes 1572872 | tf_op jit(solution)/shard_map/ppermute | solution.py:25
  311.8 3.7 collective-permute-done.43
  317.0 2.3 collective-permute-done.41.refs_12_
  320.1 1.6 collective-permute-start.44
  322.4 2.0 collective-permute-done.33
  325.7 4.7 %collective-permute-done.31.refs_4_ = bf16[512,512]{1,0:T(8,128)(2,1)S(1)} collective-permute-done((bf16[512,512]{1,0:T(8,128)(2,1)S(1)}, bf16[512,512]{1,0:T(8,128)(2,1)S(1)}, u32[]{:S(2)}, u32[]{:S(2)}) %collective-permute-start.31) | collective-permute-done | bytes 524320 | tf_op jit(solution)/shard_map/ppermute | solution.py:25
  331.3 1.6 collective-permute-start.34
  333.7 8.1 %collective-permute-done.44.refs_13_ = bf16[512,512]{1,0:T(8,128)(2,1)S(1)} collective-permute-done((bf16[512,512]{1,0:T(8,128)(2,1)S(1)}, bf16[512,512]{1,0:T(8,128)(2,1)S(1)}, u32[]{:S(2)}, u32[]{:S(2)}) %collective-permute-start.44) | collective-permute-done | bytes 524320 | tf_op jit(solution)/shard_map/ppermute | solution.py:25
  343.9 1.6 collective-permute-start.47
  346.9 6.1 %collective-permute-done.34.refs_5_ = bf16[512,512]{1,0:T(8,128)(2,1)S(1)} collective-permute-done((bf16[512,512]{1,0:T(8,128)(2,1)S(1)}, bf16[512,512]{1,0:T(8,128)(2,1)S(1)}, u32[]{:S(2)}, u32[]{:S(2)}) %collective-permute-start.34) | collective-permute-done | bytes 524320 | tf_op jit(solution)/shard_map/ppermute | solution.py:25
  353.7 5.6 %collective-permute-done.36 = bf16[512,512]{1,0:T(8,128)(2,1)S(1)} collective-permute-done((bf16[512,512]{1,0:T(8,128)(2,1)S(1)}, bf16[512,512]{1,0:T(8,128)(2,1)S(1)}, u32[]{:S(2)}, u32[]{:S(2)}) %collective-permute-start.36) | collective-permute-done | bytes 524320 | tf_op jit(solution)/shard_map/ppermute | solution.py:25
  360.7 1.6 collective-permute-start.37
  362.3 1.9 collective-permute-done.47.refs_14_
  364.9 5.5 %collective-permute-done.49 = bf16[512,512]{1,0:T(8,128)(2,1)S(1)} collective-permute-done((bf16[512,512]{1,0:T(8,128)(2,1)S(1)}, bf16[512,512]{1,0:T(8,128)(2,1)S(1)}, u32[]{:S(2)}, u32[]{:S(2)}) %collective-permute-start.49) | collective-permute-done | bytes 524320 | tf_op jit(solution)/shard_map/ppermute | solution.py:25
  371.3 1.7 collective-permute-start.50
  373.0 2.6 collective-permute-done.37.refs_6_
  377.0 1.9 collective-permute-start.40
  379.9 1.9 exp2.56
  382.9 1.9 exp2.52
  384.8 2.0 copy_bitcast_fusion
  387.0 8.7 %collective-permute-done.40.refs_7_ = bf16[512,512]{1,0:T(8,128)(2,1)} collective-permute-done((bf16[512,512]{1,0:T(8,128)(2,1)}, bf16[512,512]{1,0:T(8,128)(2,1)}, u32[]{:S(2)}, u32[]{:S(2)}) %collective-permute-start.40) | collective-permute-done | bytes 524320 | tf_op jit(solution)/shard_map/ppermute | solution.py:25
  397.7 13.2 %norm.1 = bf16[512,8192]{1,0:T(8,128)(2,1)} custom-call(s32[8]{0:T(128)S(1)} %stack.110.ids, bf16[512,512]{1,0:T(8,128)(2,1)S(1)} %get-tuple-element.91.refs_0_, bf16[512,512]{1,0:T(8,128)(2,1)S(1)} %broadcast_select_fusion.1.refs_1_, bf16[512,512]{1,0:T(8,128)(2,1)S(1)} %select_select_fusion.3.refs_2_, bf16[512,512]{1,0:T(8,128)(2,1)} %select_select_fusion.2.refs_3_, ...), custom_call_target="tpu_custom_call" | custom-call | flops 33554432 | bytes 16777216 | tf_op jit(solution)/shard_map/norm/pallas_call | solution.py:384
  (154 shorter events, 49.8 us)
Async XLA Ops:
  1.3 22.3 %collective-permute-start.12 = (bf16[512,512]{1,0:T(8,128)(2,1)S(1)}, bf16[512,512]{1,0:T(8,128)(2,1)}, u32[]{:S(2)}, u32[]{:S(2)}) collective-permute-start(bf16[512,512]{1,0:T(8,128)(2,1)S(1)} %get-tuple-element.92.refs_8_), channel_id=1, source_target_pairs={{2,0},{3,1},{4,2},{5,3},{6,4},{7,5},{10,8},{11,9},{12,10},{13,11},... | collective-permute-start | bytes 1572872 | tf_op jit(solution)/shard_map/ppermute | solution.py:25
  2.6 24.6 %collective-permute-start.11 = (bf16[512,512]{1,0:T(8,128)(2,1)S(1)}, bf16[512,512]{1,0:T(8,128)(2,1)}, u32[]{:S(2)}, u32[]{:S(2)}) collective-permute-start(bf16[512,512]{1,0:T(8,128)(2,1)S(1)} %get-tuple-element.92.refs_8_), channel_id=1, source_target_pairs={{0,2},{1,3},{2,4},{3,5},{4,6},{5,7},{8,10},{9,11},{10,12},{11,13},... | collective-permute-start | bytes 1572872 | tf_op jit(solution)/shard_map/ppermute | solution.py:25
  8.9 19.0 %collective-permute-start.10 = (bf16[512,512]{1,0:T(8,128)(2,1)S(1)}, bf16[512,512]{1,0:T(8,128)(2,1)S(1)}, u32[]{:S(2)}, u32[]{:S(2)}) collective-permute-start(bf16[512,512]{1,0:T(8,128)(2,1)S(1)} %get-tuple-element.92.refs_8_), channel_id=1, source_target_pairs={{0,1},{1,0},{2,3},{3,2},{4,5},{5,4},{6,7},{7,6},{8,9},{9,8},{10,11... | collective-permute-start | bytes 1572872 | tf_op jit(solution)/shard_map/ppermute | solution.py:25
  10.9 21.2 %collective-permute-start.2 = (bf16[512,512]{1,0:T(8,128)(2,1)S(1)}, bf16[512,512]{1,0:T(8,128)(2,1)}, u32[]{:S(2)}, u32[]{:S(2)}) collective-permute-start(bf16[512,512]{1,0:T(8,128)(2,1)S(1)} %get-tuple-element.93.refs_0_), channel_id=1, source_target_pairs={{2,0},{3,1},{4,2},{5,3},{6,4},{7,5},{10,8},{11,9},{12,10},{13,11},... | collective-permute-start | bytes 1572872 | tf_op jit(solution)/shard_map/ppermute | solution.py:25
  12.2 21.2 %collective-permute-start.1 = (bf16[512,512]{1,0:T(8,128)(2,1)S(1)}, bf16[512,512]{1,0:T(8,128)(2,1)}, u32[]{:S(2)}, u32[]{:S(2)}) collective-permute-start(bf16[512,512]{1,0:T(8,128)(2,1)S(1)} %get-tuple-element.93.refs_0_), channel_id=1, source_target_pairs={{0,2},{1,3},{2,4},{3,5},{4,6},{5,7},{8,10},{9,11},{10,12},{11,13},... | collective-permute-start | bytes 1572872 | tf_op jit(solution)/shard_map/ppermute | solution.py:25
  23.5 12.3 %collective-permute-start = (bf16[512,512]{1,0:T(8,128)(2,1)S(1)}, bf16[512,512]{1,0:T(8,128)(2,1)S(1)}, u32[]{:S(2)}, u32[]{:S(2)}) collective-permute-start(bf16[512,512]{1,0:T(8,128)(2,1)S(1)} %get-tuple-element.93.refs_0_), channel_id=1, source_target_pairs={{0,1},{1,0},{2,3},{3,2},{4,5},{5,4},{6,7},{7,6},{8,9},{9,8},{10,11... | collective-permute-start | bytes 1572872 | tf_op jit(solution)/shard_map/ppermute | solution.py:25
  27.1 17.0 %collective-permute-start.25 = (bf16[128,2048]{1,0:T(8,128)(2,1)}, bf16[128,2048]{1,0:T(8,128)(2,1)}, u32[]{:S(2)}, u32[]{:S(2)}) collective-permute-start(bf16[128,2048]{1,0:T(8,128)(2,1)} %get-tuple-element.79), channel_id=1, source_target_pairs={{0,2},{1,3},{2,4},{3,5},{4,6},{5,7},{6,0},{7,1},{8,10},{9,11},{10,... | collective-permute-start | bytes 1572872 | tf_op jit(solution)/shard_map/ppermute | solution.py:25
  28.0 26.3 %copy-start.18 = (bf16[512,512]{1,0:T(8,128)(2,1)}, bf16[512,512]{1,0:T(8,128)(2,1)S(1)}, u32[]{:S(2)}) copy-start(bf16[512,512]{1,0:T(8,128)(2,1)S(1)} %collective-permute-done.10.refs_12_) | copy-start | bytes 1572868
  28.0 26.3 %collective-permute-start.27 = (bf16[128,2048]{1,0:T(8,128)(2,1)}, bf16[128,2048]{1,0:T(8,128)(2,1)}, u32[]{:S(2)}, u32[]{:S(2)}) collective-permute-start(bf16[128,2048]{1,0:T(8,128)(2,1)} %get-tuple-element.80), channel_id=1, source_target_pairs={{0,6},{1,7},{2,0},{3,1},{4,2},{5,3},{6,4},{7,5},{8,14},{9,15},{10,... | collective-permute-start | bytes 1572872 | tf_op jit(solution)/shard_map/ppermute | solution.py:25
  32.1 49.1 %copy-start.15 = (bf16[512,512]{1,0:T(8,128)(2,1)}, bf16[512,512]{1,0:T(8,128)(2,1)S(1)}, u32[]{:S(2)}) copy-start(bf16[512,512]{1,0:T(8,128)(2,1)S(1)} %broadcast_select_fusion.2.refs_9_) | copy-start | bytes 1572868
  32.1 44.7 %collective-permute-start.26 = (bf16[128,2048]{1,0:T(8,128)(2,1)}, bf16[128,2048]{1,0:T(8,128)(2,1)}, u32[]{:S(2)}, u32[]{:S(2)}) collective-permute-start(bf16[128,2048]{1,0:T(8,128)(2,1)} %get-tuple-element.81), channel_id=1, source_target_pairs={{0,4},{1,5},{2,6},{3,7},{4,0},{5,1},{6,2},{7,3},{8,12},{9,13},{10,... | collective-permute-start | bytes 1572872 | tf_op jit(solution)/shard_map/ppermute | solution.py:25
  33.4 46.1 %collective-permute-start.14 = (bf16[512,512]{1,0:T(8,128)(2,1)}, bf16[512,512]{1,0:T(8,128)(2,1)}, u32[]{:S(2)}, u32[]{:S(2)}) collective-permute-start(bf16[512,512]{1,0:T(8,128)(2,1)} %collective-permute-done.11), channel_id=1, source_target_pairs={{2,4},{3,5},{4,6},{5,7},{10,12},{11,13},{12,14},{13,15},{18,20},{1... | collective-permute-start | bytes 1572872 | tf_op jit(solution)/shard_map/ppermute | solution.py:25
  35.9 42.4 %collective-permute-start.13 = (bf16[512,512]{1,0:T(8,128)(2,1)S(1)}, bf16[512,512]{1,0:T(8,128)(2,1)S(1)}, u32[]{:S(2)}, u32[]{:S(2)}) collective-permute-start(bf16[512,512]{1,0:T(8,128)(2,1)S(1)} %broadcast_select_fusion.2.refs_9_), channel_id=1, source_target_pairs={{0,1},{1,0},{2,3},{3,2},{4,5},{5,4},{6,7},{7,6},{8,9},{9,8},{10,11... | collective-permute-start | bytes 1572872 | tf_op jit(solution)/shard_map/ppermute | solution.py:25
  44.1 56.0 %collective-permute-start.21 = (bf16[4096,128]{1,0:T(8,128)(2,1)}, bf16[4096,128]{1,0:T(8,128)(2,1)}, u32[]{:S(2)}, u32[]{:S(2)}) collective-permute-start(bf16[4096,128]{1,0:T(8,128)(2,1)} %constant_dynamic-slice_fusion), channel_id=1, source_target_pairs={{0,8},{8,0},{1,9},{9,1},{2,10},{10,2},{3,11},{11,3},{4,12},{12,4},... | collective-permute-start | bytes 3145736 | tf_op jit(solution)/shard_map/ppermute | solution.py:25
  54.3 32.6 %collective-permute-start.15 = (bf16[512,512]{1,0:T(8,128)(2,1)}, bf16[512,512]{1,0:T(8,128)(2,1)}, u32[]{:S(2)}, u32[]{:S(2)}) collective-permute-start(bf16[512,512]{1,0:T(8,128)(2,1)} %collective-permute-done.12), channel_id=1, source_target_pairs={{2,0},{3,1},{4,2},{5,3},{10,8},{11,9},{12,10},{13,11},{18,16},{19,... | collective-permute-start | bytes 1572872 | tf_op jit(solution)/shard_map/ppermute | solution.py:25
  76.8 14.7 %collective-permute-start.4 = (bf16[512,512]{1,0:T(8,128)(2,1)}, bf16[512,512]{1,0:T(8,128)(2,1)}, u32[]{:S(2)}, u32[]{:S(2)}) collective-permute-start(bf16[512,512]{1,0:T(8,128)(2,1)} %collective-permute-done.1), channel_id=1, source_target_pairs={{2,4},{3,5},{4,6},{5,7},{10,12},{11,13},{12,14},{13,15},{18,20},{1... | collective-permute-start | bytes 1572872 | tf_op jit(solution)/shard_map/ppermute | solution.py:25
  78.3 19.9 %collective-permute-start.5 = (bf16[512,512]{1,0:T(8,128)(2,1)}, bf16[512,512]{1,0:T(8,128)(2,1)}, u32[]{:S(2)}, u32[]{:S(2)}) collective-permute-start(bf16[512,512]{1,0:T(8,128)(2,1)} %collective-permute-done.2), channel_id=1, source_target_pairs={{2,0},{3,1},{4,2},{5,3},{10,8},{11,9},{12,10},{13,11},{18,16},{19,... | collective-permute-start | bytes 1572872 | tf_op jit(solution)/shard_map/ppermute | solution.py:25
  79.6 11.9 %collective-permute-start.3 = (bf16[512,512]{1,0:T(8,128)(2,1)S(1)}, bf16[512,512]{1,0:T(8,128)(2,1)S(1)}, u32[]{:S(2)}, u32[]{:S(2)}) collective-permute-start(bf16[512,512]{1,0:T(8,128)(2,1)S(1)} %broadcast_select_fusion.3.refs_1_), channel_id=1, source_target_pairs={{0,1},{1,0},{2,3},{3,2},{4,5},{5,4},{6,7},{7,6},{8,9},{9,8},{10,11... | collective-permute-start | bytes 1572872 | tf_op jit(solution)/shard_map/ppermute | solution.py:25
  86.9 36.7 %collective-permute-start.28 = (bf16[3,128,2048]{2,1,0:T(8,128)(2,1)}, bf16[3,128,2048]{2,1,0:T(8,128)(2,1)}, u32[]{:S(2)}, u32[]{:S(2)}) collective-permute-start(bf16[3,128,2048]{2,1,0:T(8,128)(2,1)} %pad_maximum_fusion.4), channel_id=1, source_target_pairs={{0,16},{16,0},{1,17},{17,1},{2,18},{18,2},{3,19},{19,3},{4,20},{20... | collective-permute-start | bytes 4718600 | tf_op jit(solution)/shard_map/ppermute | solution.py:25
  91.4 37.7 %collective-permute-start.20 = (bf16[4096,128]{1,0:T(8,128)(2,1)}, bf16[4096,128]{1,0:T(8,128)(2,1)S(1)}, u32[]{:S(2)}, u32[]{:S(2)}) collective-permute-start(bf16[4096,128]{1,0:T(8,128)(2,1)} %constant_dynamic-slice_fusion.1), channel_id=1, source_target_pairs={{0,8},{8,0},{1,9},{9,1},{2,10},{10,2},{3,11},{11,3},{4,12},{12,4},... | collective-permute-start | bytes 3145736 | tf_op jit(solution)/shard_map/ppermute | solution.py:25
  91.4 46.8 %collective-permute-start.18 = (bf16[512,512]{1,0:T(8,128)(2,1)}, bf16[512,512]{1,0:T(8,128)(2,1)S(1)}, u32[]{:S(2)}, u32[]{:S(2)}) collective-permute-start(bf16[512,512]{1,0:T(8,128)(2,1)} %collective-permute-done.15), channel_id=1, source_target_pairs={{2,0},{3,1},{10,8},{11,9},{18,16},{19,17},{26,24},{27,25}} | collective-permute-start | bytes 1572872 | tf_op jit(solution)/shard_map/ppermute | solution.py:25
  98.2 41.7 %collective-permute-start.17 = (bf16[512,512]{1,0:T(8,128)(2,1)}, bf16[512,512]{1,0:T(8,128)(2,1)S(1)}, u32[]{:S(2)}, u32[]{:S(2)}) collective-permute-start(bf16[512,512]{1,0:T(8,128)(2,1)} %collective-permute-done.14), channel_id=1, source_target_pairs={{4,6},{5,7},{12,14},{13,15},{20,22},{21,23},{28,30},{29,31}} | collective-permute-start | bytes 1572872 | tf_op jit(solution)/shard_map/ppermute | solution.py:25
  100.1 23.5 %copy-start.16 = (bf16[512,512]{1,0:T(8,128)(2,1)}, bf16[512,512]{1,0:T(8,128)(2,1)S(1)}, u32[]{:S(2)}) copy-start(bf16[512,512]{1,0:T(8,128)(2,1)S(1)} %select_select_fusion.5.refs_10_) | copy-start | bytes 1572868
  100.1 51.4 %collective-permute-start.8 = (bf16[512,512]{1,0:T(8,128)(2,1)}, bf16[512,512]{1,0:T(8,128)(2,1)S(1)}, u32[]{:S(2)}, u32[]{:S(2)}) collective-permute-start(bf16[512,512]{1,0:T(8,128)(2,1)} %collective-permute-done.5), channel_id=1, source_target_pairs={{2,0},{3,1},{10,8},{11,9},{18,16},{19,17},{26,24},{27,25}} | collective-permute-start | bytes 1572872 | tf_op jit(solution)/shard_map/ppermute | solution.py:25
  123.6 13.1 %collective-permute-start.16 = (bf16[512,512]{1,0:T(8,128)(2,1)S(1)}, bf16[512,512]{1,0:T(8,128)(2,1)S(1)}, u32[]{:S(2)}, u32[]{:S(2)}) collective-permute-start(bf16[512,512]{1,0:T(8,128)(2,1)S(1)} %select_select_fusion.5.refs_10_), channel_id=1, source_target_pairs={{0,1},{1,0},{2,3},{3,2},{4,5},{5,4},{6,7},{7,6},{8,9},{9,8},{10,11... | collective-permute-start | bytes 1572872 | tf_op jit(solution)/shard_map/ppermute | solution.py:25
  129.2 22.4 %collective-permute-start.7 = (bf16[512,512]{1,0:T(8,128)(2,1)}, bf16[512,512]{1,0:T(8,128)(2,1)S(1)}, u32[]{:S(2)}, u32[]{:S(2)}) collective-permute-start(bf16[512,512]{1,0:T(8,128)(2,1)} %collective-permute-done.4), channel_id=1, source_target_pairs={{4,6},{5,7},{12,14},{13,15},{20,22},{21,23},{28,30},{29,31}} | collective-permute-start | bytes 1572872 | tf_op jit(solution)/shard_map/ppermute | solution.py:25
  136.7 14.9 %collective-permute-start.6 = (bf16[512,512]{1,0:T(8,128)(2,1)S(1)}, bf16[512,512]{1,0:T(8,128)(2,1)S(1)}, u32[]{:S(2)}, u32[]{:S(2)}) collective-permute-start(bf16[512,512]{1,0:T(8,128)(2,1)S(1)} %select_select_fusion.7.refs_2_), channel_id=1, source_target_pairs={{0,1},{1,0},{2,3},{3,2},{4,5},{5,4},{6,7},{7,6},{8,9},{9,8},{10,11... | collective-permute-start | bytes 1572872 | tf_op jit(solution)/shard_map/ppermute | solution.py:25
  138.2 81.8 %collective-permute-start.29 = (bf16[2,3,128,2048]{3,2,1,0:T(8,128)(2,1)}, bf16[2,3,128,2048]{3,2,1,0:T(8,128)(2,1)}, u32[]{:S(2)}, u32[]{:S(2)}) collective-permute-start(bf16[2,3,128,2048]{3,2,1,0:T(8,128)(2,1)} %pad_maximum_fusion.1), channel_id=1, source_target_pairs={{0,8},{8,0},{1,9},{9,1},{2,10},{10,2},{3,11},{11,3},{4,12},{12,4},... | collective-permute-start | bytes 9437192 | tf_op jit(solution)/shard_map/ppermute | solution.py:25
  140.1 13.5 %copy-start.17 = (bf16[512,512]{1,0:T(8,128)(2,1)}, bf16[512,512]{1,0:T(8,128)(2,1)S(1)}, u32[]{:S(2)}) copy-start(bf16[512,512]{1,0:T(8,128)(2,1)S(1)} %select_select_fusion.4.refs_11_) | copy-start | bytes 1572868
  140.1 22.7 %collective-permute-start.19 = (bf16[512,512]{1,0:T(8,128)(2,1)S(1)}, bf16[512,512]{1,0:T(8,128)(2,1)S(1)}, u32[]{:S(2)}, u32[]{:S(2)}) collective-permute-start(bf16[512,512]{1,0:T(8,128)(2,1)S(1)} %select_select_fusion.4.refs_11_), channel_id=1, source_target_pairs={{0,1},{1,0},{2,3},{3,2},{4,5},{5,4},{6,7},{7,6},{8,9},{9,8},{10,11... | collective-permute-start | bytes 1572872 | tf_op jit(solution)/shard_map/ppermute | solution.py:25
  151.8 19.6 %collective-permute-start.9 = (bf16[512,512]{1,0:T(8,128)(2,1)S(1)}, bf16[512,512]{1,0:T(8,128)(2,1)S(1)}, u32[]{:S(2)}, u32[]{:S(2)}) collective-permute-start(bf16[512,512]{1,0:T(8,128)(2,1)S(1)} %select_select_fusion.6.refs_3_), channel_id=1, source_target_pairs={{0,1},{1,0},{2,3},{3,2},{4,5},{5,4},{6,7},{7,6},{8,9},{9,8},{10,11... | collective-permute-start | bytes 1572872 | tf_op jit(solution)/shard_map/ppermute | solution.py:25
  214.5 13.8 %collective-permute-start.24 = (bf16[512,512]{1,0:T(8,128)(2,1)S(1)}, bf16[512,512]{1,0:T(8,128)(2,1)S(1)}, u32[]{:S(2)}, u32[]{:S(2)}) collective-permute-start(bf16[512,512]{1,0:T(8,128)(2,1)S(1)} %attend.1.refs_0_), channel_id=1, source_target_pairs={{0,6},{1,7},{2,0},{3,1},{4,2},{5,3},{6,4},{7,5},{8,14},{9,15},{10,... | collective-permute-start | bytes 1572872 | tf_op jit(solution)/shard_map/ppermute | solution.py:25
  214.6 49.4 %collective-permute-start.23 = (bf16[512,512]{1,0:T(8,128)(2,1)S(1)}, bf16[512,512]{1,0:T(8,128)(2,1)S(1)}, u32[]{:S(2)}, u32[]{:S(2)}) collective-permute-start(bf16[512,512]{1,0:T(8,128)(2,1)S(1)} %attend.1.refs_0_), channel_id=1, source_target_pairs={{0,4},{1,5},{2,6},{3,7},{4,0},{5,1},{6,2},{7,3},{8,12},{9,13},{10,... | collective-permute-start | bytes 1572872 | tf_op jit(solution)/shard_map/ppermute | solution.py:25
  218.1 45.9 %collective-permute-start.22 = (bf16[512,512]{1,0:T(8,128)(2,1)S(1)}, bf16[512,512]{1,0:T(8,128)(2,1)S(1)}, u32[]{:S(2)}, u32[]{:S(2)}) collective-permute-start(bf16[512,512]{1,0:T(8,128)(2,1)S(1)} %attend.1.refs_0_), channel_id=1, source_target_pairs={{0,2},{1,3},{2,4},{3,5},{4,6},{5,7},{6,0},{7,1},{8,10},{9,11},{10,... | collective-permute-start | bytes 1572872 | tf_op jit(solution)/shard_map/ppermute | solution.py:25
  222.2 41.8 %copy-start.1 = (bf16[256,256]{1,0:T(8,128)(2,1)S(1)}, bf16[256,256]{1,0:T(8,128)(2,1)}, u32[]{:S(2)}) copy-start(bf16[256,256]{1,0:T(8,128)(2,1)} %constant.147.clone.1.refs_6_.table) | copy-start | bytes 393220
  222.2 41.8 %copy-start.14 = (f32[2,8,8,128]{3,1,2,0:T(8,128)S(1)}, f32[2,8,8,128]{3,1,2,0:T(8,128)}, u32[]{:S(2)}) copy-start(f32[2,8,8,128]{3,1,2,0:T(8,128)} %copy.25) | copy-start | bytes 196612
  272.7 24.9 %collective-permute-start.30 = (bf16[512,1024]{1,0:T(8,128)(2,1)}, bf16[512,1024]{1,0:T(8,128)(2,1)S(1)}, u32[]{:S(2)}, u32[]{:S(2)}) collective-permute-start(bf16[512,1024]{1,0:T(8,128)(2,1)} %code_terms.3), channel_id=1, source_target_pairs={{0,1},{1,0},{2,3},{3,2},{4,5},{5,4},{6,7},{7,6},{8,9},{9,8},{10,11... | collective-permute-start | bytes 3145736 | tf_op jit(solution)/shard_map/ppermute | solution.py:25
  273.9 23.7 %copy-start = (bf16[512,1024]{1,0:T(8,128)(2,1)S(1)}, bf16[512,1024]{1,0:T(8,128)(2,1)}, u32[]{:S(2)}) copy-start(bf16[512,1024]{1,0:T(8,128)(2,1)} %hidden.1) | copy-start | bytes 3145732
  298.8 16.8 %collective-permute-start.43 = (bf16[512,512]{1,0:T(8,128)(2,1)S(1)}, bf16[512,512]{1,0:T(8,128)(2,1)S(1)}, u32[]{:S(2)}, u32[]{:S(2)}) collective-permute-start(bf16[512,512]{1,0:T(8,128)(2,1)S(1)} %get-tuple-element.90.refs_8_), channel_id=1, source_target_pairs={{2,0},{3,1},{4,2},{5,3},{6,4},{7,5},{10,8},{11,9},{12,10},{13,11},... | collective-permute-start | bytes 1572872 | tf_op jit(solution)/shard_map/ppermute | solution.py:25
  300.1 16.9 %collective-permute-start.42 = (bf16[512,512]{1,0:T(8,128)(2,1)S(1)}, bf16[512,512]{1,0:T(8,128)(2,1)S(1)}, u32[]{:S(2)}, u32[]{:S(2)}) collective-permute-start(bf16[512,512]{1,0:T(8,128)(2,1)S(1)} %get-tuple-element.90.refs_8_), channel_id=1, source_target_pairs={{0,2},{1,3},{2,4},{3,5},{4,6},{5,7},{8,10},{9,11},{10,12},{11,13},... | collective-permute-start | bytes 1572872 | tf_op jit(solution)/shard_map/ppermute | solution.py:25
  304.6 14.6 %collective-permute-start.41 = (bf16[512,512]{1,0:T(8,128)(2,1)S(1)}, bf16[512,512]{1,0:T(8,128)(2,1)S(1)}, u32[]{:S(2)}, u32[]{:S(2)}) collective-permute-start(bf16[512,512]{1,0:T(8,128)(2,1)S(1)} %get-tuple-element.90.refs_8_), channel_id=1, source_target_pairs={{0,1},{1,0},{2,3},{3,2},{4,5},{5,4},{6,7},{7,6},{8,9},{9,8},{10,11... | collective-permute-start | bytes 1572872 | tf_op jit(solution)/shard_map/ppermute | solution.py:25
  306.0 18.5 %collective-permute-start.33 = (bf16[512,512]{1,0:T(8,128)(2,1)S(1)}, bf16[512,512]{1,0:T(8,128)(2,1)S(1)}, u32[]{:S(2)}, u32[]{:S(2)}) collective-permute-start(bf16[512,512]{1,0:T(8,128)(2,1)S(1)} %get-tuple-element.91.refs_0_), channel_id=1, source_target_pairs={{2,0},{3,1},{4,2},{5,3},{6,4},{7,5},{10,8},{11,9},{12,10},{13,11},... | collective-permute-start | bytes 1572872 | tf_op jit(solution)/shard_map/ppermute | solution.py:25
  307.3 18.5 %collective-permute-start.32 = (bf16[512,512]{1,0:T(8,128)(2,1)S(1)}, bf16[512,512]{1,0:T(8,128)(2,1)S(1)}, u32[]{:S(2)}, u32[]{:S(2)}) collective-permute-start(bf16[512,512]{1,0:T(8,128)(2,1)S(1)} %get-tuple-element.91.refs_0_), channel_id=1, source_target_pairs={{0,2},{1,3},{2,4},{3,5},{4,6},{5,7},{8,10},{9,11},{10,12},{11,13},... | collective-permute-start | bytes 1572872 | tf_op jit(solution)/shard_map/ppermute | solution.py:25
  315.5 15.0 %collective-permute-start.31 = (bf16[512,512]{1,0:T(8,128)(2,1)S(1)}, bf16[512,512]{1,0:T(8,128)(2,1)S(1)}, u32[]{:S(2)}, u32[]{:S(2)}) collective-permute-start(bf16[512,512]{1,0:T(8,128)(2,1)S(1)} %get-tuple-element.91.refs_0_), channel_id=1, source_target_pairs={{0,1},{1,0},{2,3},{3,2},{4,5},{5,4},{6,7},{7,6},{8,9},{9,8},{10,11... | collective-permute-start | bytes 1572872 | tf_op jit(solution)/shard_map/ppermute | solution.py:25
  320.1 21.6 %collective-permute-start.44 = (bf16[512,512]{1,0:T(8,128)(2,1)S(1)}, bf16[512,512]{1,0:T(8,128)(2,1)S(1)}, u32[]{:S(2)}, u32[]{:S(2)}) collective-permute-start(bf16[512,512]{1,0:T(8,128)(2,1)S(1)} %broadcast_select_fusion.refs_9_), channel_id=1, source_target_pairs={{0,1},{1,0},{2,3},{3,2},{4,5},{5,4},{6,7},{7,6},{8,9},{9,8},{10,11... | collective-permute-start | bytes 1572872 | tf_op jit(solution)/shard_map/ppermute | solution.py:25
  321.7 22.1 %collective-permute-start.45 = (bf16[512,512]{1,0:T(8,128)(2,1)S(1)}, bf16[512,512]{1,0:T(8,128)(2,1)S(1)}, u32[]{:S(2)}, u32[]{:S(2)}) collective-permute-start(bf16[512,512]{1,0:T(8,128)(2,1)S(1)} %collective-permute-done.42), channel_id=1, source_target_pairs={{2,4},{3,5},{4,6},{5,7},{10,12},{11,13},{12,14},{13,15},{18,20},{1... | collective-permute-start | bytes 1572872 | tf_op jit(solution)/shard_map/ppermute | solution.py:25
  324.4 19.4 %collective-permute-start.46 = (bf16[512,512]{1,0:T(8,128)(2,1)S(1)}, bf16[512,512]{1,0:T(8,128)(2,1)S(1)}, u32[]{:S(2)}, u32[]{:S(2)}) collective-permute-start(bf16[512,512]{1,0:T(8,128)(2,1)S(1)} %collective-permute-done.43), channel_id=1, source_target_pairs={{2,0},{3,1},{4,2},{5,3},{10,8},{11,9},{12,10},{13,11},{18,16},{19,... | collective-permute-start | bytes 1572872 | tf_op jit(solution)/shard_map/ppermute | solution.py:25
  331.3 21.6 %collective-permute-start.34 = (bf16[512,512]{1,0:T(8,128)(2,1)S(1)}, bf16[512,512]{1,0:T(8,128)(2,1)S(1)}, u32[]{:S(2)}, u32[]{:S(2)}) collective-permute-start(bf16[512,512]{1,0:T(8,128)(2,1)S(1)} %broadcast_select_fusion.1.refs_1_), channel_id=1, source_target_pairs={{0,1},{1,0},{2,3},{3,2},{4,5},{5,4},{6,7},{7,6},{8,9},{9,8},{10,11... | collective-permute-start | bytes 1572872 | tf_op jit(solution)/shard_map/ppermute | solution.py:25
  333.0 20.7 %collective-permute-start.35 = (bf16[512,512]{1,0:T(8,128)(2,1)S(1)}, bf16[512,512]{1,0:T(8,128)(2,1)S(1)}, u32[]{:S(2)}, u32[]{:S(2)}) collective-permute-start(bf16[512,512]{1,0:T(8,128)(2,1)S(1)} %collective-permute-done.32), channel_id=1, source_target_pairs={{2,4},{3,5},{4,6},{5,7},{10,12},{11,13},{12,14},{13,15},{18,20},{1... | collective-permute-start | bytes 1572872 | tf_op jit(solution)/shard_map/ppermute | solution.py:25
  342.5 16.7 %collective-permute-start.36 = (bf16[512,512]{1,0:T(8,128)(2,1)S(1)}, bf16[512,512]{1,0:T(8,128)(2,1)S(1)}, u32[]{:S(2)}, u32[]{:S(2)}) collective-permute-start(bf16[512,512]{1,0:T(8,128)(2,1)S(1)} %collective-permute-done.33), channel_id=1, source_target_pairs={{2,0},{3,1},{4,2},{5,3},{10,8},{11,9},{12,10},{13,11},{18,16},{19,... | collective-permute-start | bytes 1572872 | tf_op jit(solution)/shard_map/ppermute | solution.py:25
  343.9 20.3 %collective-permute-start.47 = (bf16[512,512]{1,0:T(8,128)(2,1)S(1)}, bf16[512,512]{1,0:T(8,128)(2,1)S(1)}, u32[]{:S(2)}, u32[]{:S(2)}) collective-permute-start(bf16[512,512]{1,0:T(8,128)(2,1)S(1)} %select_select_fusion.1.refs_10_), channel_id=1, source_target_pairs={{0,1},{1,0},{2,3},{3,2},{4,5},{5,4},{6,7},{7,6},{8,9},{9,8},{10,11... | collective-permute-start | bytes 1572872 | tf_op jit(solution)/shard_map/ppermute | solution.py:25
  345.6 24.9 %collective-permute-start.49 = (bf16[512,512]{1,0:T(8,128)(2,1)S(1)}, bf16[512,512]{1,0:T(8,128)(2,1)S(1)}, u32[]{:S(2)}, u32[]{:S(2)}) collective-permute-start(bf16[512,512]{1,0:T(8,128)(2,1)S(1)} %collective-permute-done.46), channel_id=1, source_target_pairs={{2,0},{3,1},{10,8},{11,9},{18,16},{19,17},{26,24},{27,25}} | collective-permute-start | bytes 1572872 | tf_op jit(solution)/shard_map/ppermute | solution.py:25
  353.0 18.4 %copy-start.8 = (bf16[512,512]{1,0:T(8,128)(2,1)}, bf16[512,512]{1,0:T(8,128)(2,1)S(1)}, u32[]{:S(2)}) copy-start(bf16[512,512]{1,0:T(8,128)(2,1)S(1)} %collective-permute-done.34.refs_5_) | copy-start | bytes 1572868
  353.0 17.5 %collective-permute-start.48 = (bf16[512,512]{1,0:T(8,128)(2,1)S(1)}, bf16[512,512]{1,0:T(8,128)(2,1)S(1)}, u32[]{:S(2)}, u32[]{:S(2)}) collective-permute-start(bf16[512,512]{1,0:T(8,128)(2,1)S(1)} %collective-permute-done.45), channel_id=1, source_target_pairs={{4,6},{5,7},{12,14},{13,15},{20,22},{21,23},{28,30},{29,31}} | collective-permute-start | bytes 1572872 | tf_op jit(solution)/shard_map/ppermute | solution.py:25
  359.3 16.8 %collective-permute-start.39 = (bf16[512,512]{1,0:T(8,128)(2,1)S(1)}, bf16[512,512]{1,0:T(8,128)(2,1)S(1)}, u32[]{:S(2)}, u32[]{:S(2)}) collective-permute-start(bf16[512,512]{1,0:T(8,128)(2,1)S(1)} %collective-permute-done.36), channel_id=1, source_target_pairs={{2,0},{3,1},{10,8},{11,9},{18,16},{19,17},{26,24},{27,25}} | collective-permute-start | bytes 1572872 | tf_op jit(solution)/shard_map/ppermute | solution.py:25
  360.7 18.2 %copy-start.27 = (bf16[8192]{0:T(1024)(128)(2,1)S(1)}, bf16[8192]{0:T(1024)(128)(2,1)}, u32[]{:S(2)}) copy-start(bf16[8192]{0:T(1024)(128)(2,1)} %param.20) | copy-start | bytes 49156
  360.7 18.2 %copy-start.28 = (s32[16,64]{1,0:T(8,128)S(1)}, s32[16,64]{1,0:T(8,128)}, u32[]{:S(2)}) copy-start(s32[16,64]{1,0:T(8,128)} %param.21) | copy-start | bytes 12292
  360.7 14.9 %collective-permute-start.37 = (bf16[512,512]{1,0:T(8,128)(2,1)S(1)}, bf16[512,512]{1,0:T(8,128)(2,1)S(1)}, u32[]{:S(2)}, u32[]{:S(2)}) collective-permute-start(bf16[512,512]{1,0:T(8,128)(2,1)S(1)} %select_select_fusion.3.refs_2_), channel_id=1, source_target_pairs={{0,1},{1,0},{2,3},{3,2},{4,5},{5,4},{6,7},{7,6},{8,9},{9,8},{10,11... | collective-permute-start | bytes 1572872 | tf_op jit(solution)/shard_map/ppermute | solution.py:25
  364.2 12.8 %copy-start.10 = (bf16[512,512]{1,0:T(8,128)(2,1)}, bf16[512,512]{1,0:T(8,128)(2,1)S(1)}, u32[]{:S(2)}) copy-start(bf16[512,512]{1,0:T(8,128)(2,1)S(1)} %collective-permute-done.47.refs_14_) | copy-start | bytes 1572868
  364.2 11.9 %collective-permute-start.38 = (bf16[512,512]{1,0:T(8,128)(2,1)S(1)}, bf16[512,512]{1,0:T(8,128)(2,1)S(1)}, u32[]{:S(2)}, u32[]{:S(2)}) collective-permute-start(bf16[512,512]{1,0:T(8,128)(2,1)S(1)} %collective-permute-done.35), channel_id=1, source_target_pairs={{4,6},{5,7},{12,14},{13,15},{20,22},{21,23},{28,30},{29,31}} | collective-permute-start | bytes 1572872 | tf_op jit(solution)/shard_map/ppermute | solution.py:25
  371.3 15.6 %collective-permute-start.50 = (bf16[512,512]{1,0:T(8,128)(2,1)}, bf16[512,512]{1,0:T(8,128)(2,1)}, u32[]{:S(2)}, u32[]{:S(2)}) collective-permute-start(bf16[512,512]{1,0:T(8,128)(2,1)} %select_select_fusion.refs_11_), channel_id=1, source_target_pairs={{0,1},{1,0},{2,3},{3,2},{4,5},{5,4},{6,7},{7,6},{8,9},{9,8},{10,11... | collective-permute-start | bytes 1572872 | tf_op jit(solution)/shard_map/ppermute | solution.py:25
  377.0 18.7 %collective-permute-start.40 = (bf16[512,512]{1,0:T(8,128)(2,1)}, bf16[512,512]{1,0:T(8,128)(2,1)}, u32[]{:S(2)}, u32[]{:S(2)}) collective-permute-start(bf16[512,512]{1,0:T(8,128)(2,1)} %select_select_fusion.2.refs_3_), channel_id=1, source_target_pairs={{0,1},{1,0},{2,3},{3,2},{4,5},{5,4},{6,7},{7,6},{8,9},{9,8},{10,11... | collective-permute-start | bytes 1572872 | tf_op jit(solution)/shard_map/ppermute | solution.py:25
  384.8 10.8 %copy-start.7 = (bf16[512,512]{1,0:T(8,128)(2,1)S(1)}, bf16[512,512]{1,0:T(8,128)(2,1)}, u32[]{:S(2)}) copy-start(bf16[512,512]{1,0:T(8,128)(2,1)} %copy-done.6) | copy-start | bytes 1572868
  384.8 10.8 %copy-start.9 = (bf16[512,512]{1,0:T(8,128)(2,1)S(1)}, bf16[512,512]{1,0:T(8,128)(2,1)}, u32[]{:S(2)}) copy-start(bf16[512,512]{1,0:T(8,128)(2,1)} %copy-done.8) | copy-start | bytes 1572868
  (16 other events, 79.8 us)
